TPU v7x, 256 devices: a whole 4x4x8 slice. The times are simulated.
256 devices in a mesh: ctx: 32 (over x, y, core), fsdp: 8 (over z).
Axes of the slice: x: 4, y: 4, z: 8, core: 2. Of those that a mesh axis runs over, the one named last changes fastest.
Arguments:
- query_mr: bfloat16 [4096, 4096], P('ctx', 'fsdp'), may hold values from -6 to 6
- key_mr: bfloat16 [4096, 4096], P('ctx', 'fsdp'), may hold values from -6 to 6
- value_mr: bfloat16 [4096, 4096], P('ctx', 'fsdp'), may hold values from -6 to 6
- query_li: bfloat16 [4096, 4096], P('ctx', 'fsdp'), may hold values from -6 to 6
- key_li: bfloat16 [4096, 4096], P('ctx', 'fsdp'), may hold values from -6 to 6
- mr_taps: float32 [128, 4096], P(None, 'fsdp'), may hold values from -0.5 to 0.5
- li_time: float32 [16, 4096], P(None, 'fsdp'), may hold values from 30 to 81920
- li_residue: float32 [16, 4096], P(None, 'fsdp'), may hold values from -5 to 5
- li_skip: float32 [4096], P('fsdp'), may hold values from -6 to 6
- out_weight: bfloat16 [4096, 4096], P('ctx', 'fsdp'), may hold values from -0.09375 to 0.09375
- cotangent: bfloat16 [4096, 4096], P('ctx', 'fsdp'), may hold values from -6 to 6
Outputs:
- output: float32 [4096, 4096], P('ctx', 'fsdp')
- grad_query_mr: float32 [4096, 4096], P('ctx', 'fsdp')
- grad_key_mr: float32 [4096, 4096], P('ctx', 'fsdp')
- grad_value_mr: float32 [4096, 4096], P('ctx', 'fsdp')
- grad_query_li: float32 [4096, 4096], P('ctx', 'fsdp')
- grad_key_li: float32 [4096, 4096], P('ctx', 'fsdp')
- grad_taps: float32 [128, 4096], P(None, 'fsdp')
- grad_weight: float32 [4096, 4096], P('ctx', 'fsdp')
All inputs are finite; a program needn't handle non-finite values.
Results may differ from a plain program's by a relative error of at most 0.014.
Values may be sent and summed in bfloat16 or wider, within the bound.
A program may use at most 64 MiB of HBM per device.

v0:
```python
import math

import jax
import jax.numpy as jnp
from jax import lax
from jax.sharding import PartitionSpec as P


def shifted(x, axis, by):
    size = lax.axis_size(axis)
    pairs = [(i, i + by) for i in range(size) if 0 <= i + by < size]
    return lax.ppermute(x, axis, pairs)


def entering(x, axis, combine, identity, reverse):
    size, here = (lax.axis_size(axis), lax.axis_index(axis))
    everything = jax.tree.map(lambda part: lax.all_gather(part, axis), x)
    start = jax.tree.map(
        lambda part, zero: jnp.broadcast_to(jnp.asarray(zero, part.dtype), part.shape), x, identity
    )

    def lap(k, before):
        at = size - 1 - k if reverse else k
        reached = at > here if reverse else at < here
        new = combine(before, jax.tree.map(lambda part: part[at], everything))
        return jax.tree.map(lambda a, b: jnp.where(reached, a, b), new, before)

    return lax.fori_loop(0, size, lap, start)


def compose(earlier, latter):
    return (earlier[0] * latter[0], latter[0] * earlier[1] + latter[1])


def tap_sum(padded, tap_weights, row_count, backward):
    rim_size = tap_weights.shape[0] - 1
    group_count = tap_weights.shape[0] // 8

    def one_turn(group_id, running):
        for within in range(8):
            tap_index = group_id * 8 + within
            if backward:
                first_row = tap_index
            else:
                first_row = rim_size - tap_index
            window = lax.dynamic_slice_in_dim(padded, first_row, row_count, 0).astype(jnp.float32)
            weight_row = lax.dynamic_index_in_dim(tap_weights, tap_index, 0, keepdims=False)
            running = running + weight_row[None, :] * window
        return running

    return lax.fori_loop(
        0, group_count, one_turn, jnp.zeros((row_count, padded.shape[1]), jnp.float32)
    )


def tap_gradient(grad_conv, padded, tap_count):
    row_count = grad_conv.shape[0]
    rim_size = tap_count - 1

    def one_group(group_id):
        sums = []
        for within in range(8):
            tap_index = group_id * 8 + within
            window = lax.dynamic_slice_in_dim(padded, rim_size - tap_index, row_count, 0).astype(
                jnp.float32
            )
            sums.append(jnp.sum(grad_conv * window, axis=0))
        return jnp.stack(sums)

    stacked = lax.map(one_group, jnp.arange(tap_count // 8, dtype=jnp.int32))
    return stacked.reshape(tap_count, grad_conv.shape[1])


def end_state(signal, rate, block_len):
    block_count = signal.shape[0] // block_len
    blocks = signal.reshape(block_count, block_len, signal.shape[1])
    places = jnp.arange(block_len, dtype=jnp.float32)
    tail_weights = jnp.exp(-rate[None] * (block_len - 1 - places)[:, None, None])
    stride = jnp.exp(-rate * block_len)

    def fold_block(carried, block_rows):
        added = jnp.einsum("jc,jmc->mc", block_rows, tail_weights, precision=lax.Precision.HIGHEST)
        return (stride * carried + added, None)

    closing, unused = lax.scan(fold_block, jnp.zeros(rate.shape, jnp.float32), blocks)
    return closing


def modal_output(signal, rate, mode_coef, incoming, block_len):
    block_count = signal.shape[0] // block_len
    blocks = signal.reshape(block_count, block_len, signal.shape[1])
    places = jnp.arange(block_len, dtype=jnp.float32)
    lower = (places[:, None] >= places[None, :]).astype(jnp.float32)
    rising = jnp.exp(rate[None] * places[:, None, None])
    falling = jnp.exp(-rate[None] * places[:, None, None])
    after_start = jnp.exp(-rate[None] * (places + 1.0)[:, None, None])

    def emit_block(carried, block_rows):
        scaled = block_rows[:, None, :] * rising
        summed = jnp.dot(
            lower, scaled.reshape(block_len, -1), precision=lax.Precision.HIGHEST
        ).reshape(scaled.shape)
        states = summed * falling + after_start * carried[None]
        return (states[-1], jnp.sum(states * mode_coef[None], axis=1))

    closing, outputs = lax.scan(emit_block, incoming, blocks)
    return outputs.reshape(signal.shape)


def shards(
    query_mr,
    key_mr,
    value_mr,
    query_li,
    key_li,
    mr_taps,
    li_time,
    li_residue,
    li_skip,
    out_weight,
    cotangent,
):
    row_count = query_mr.shape[0]
    rim_size = mr_taps.shape[0] - 1
    block_len = min(64, row_count)
    ctx_count = lax.axis_size("ctx")
    grad_scale = 1.0 / math.sqrt(row_count * ctx_count)
    rate = 1.0 / li_time
    mode_coef = li_residue * jnp.sqrt(-jnp.expm1(-2.0 * rate))
    device_decay = jnp.exp(-rate * row_count)
    mr_product = (key_mr.astype(jnp.float32) * value_mr.astype(jnp.float32)).astype(jnp.bfloat16)
    before = shifted(mr_product[row_count - rim_size :], "ctx", 1)
    padded = jnp.concatenate([before, mr_product], axis=0)
    mr_conv = tap_sum(padded, mr_taps, row_count, False)
    mixed_mr = (query_mr.astype(jnp.float32) * mr_conv).astype(jnp.bfloat16)
    li_input = (key_li.astype(jnp.float32) * mixed_mr.astype(jnp.float32)).astype(jnp.bfloat16)
    li_signal = li_input.astype(jnp.float32)
    local_end = end_state(li_signal, rate, block_len)
    unused_decay, incoming = entering(
        (device_decay, local_end),
        "ctx",
        compose,
        (jnp.ones_like(device_decay), jnp.zeros_like(local_end)),
        False,
    )
    li_out = li_skip[None, :] * li_signal + modal_output(
        li_signal, rate, mode_coef, incoming, block_len
    )
    mixed_li = (query_li.astype(jnp.float32) * li_out).astype(jnp.bfloat16)
    partial_out = lax.dot_general(
        mixed_li,
        lax.all_gather(out_weight, "ctx", axis=0, tiled=True),
        (((1,), (1,)), ((), ())),
        preferred_element_type=jnp.float32,
    )
    output = lax.psum_scatter(partial_out, "fsdp", scatter_dimension=1, tiled=True)
    full_cot = lax.all_gather(cotangent, "fsdp", axis=1, tiled=True)
    columns = full_cot
    grad_mixed = jnp.dot(
        columns,
        lax.all_gather(out_weight, "ctx", axis=0, tiled=True),
        preferred_element_type=jnp.float32,
    )
    grad_query_li = grad_mixed * li_out
    grad_li_out = grad_mixed * query_li.astype(jnp.float32)
    flipped = grad_li_out[::-1]
    back_end = end_state(flipped, rate, block_len)
    unused_back, back_in = entering(
        (device_decay, back_end),
        "ctx",
        compose,
        (jnp.ones_like(device_decay), jnp.zeros_like(back_end)),
        True,
    )
    grad_li_input = (
        li_skip[None, :] * grad_li_out
        + modal_output(flipped, rate, mode_coef, back_in, block_len)[::-1]
    )
    grad_key_li = grad_li_input * mixed_mr.astype(jnp.float32)
    grad_mixed_mr = grad_li_input * key_li.astype(jnp.float32)
    grad_query_mr = grad_mixed_mr * mr_conv
    grad_conv = grad_mixed_mr * query_mr.astype(jnp.float32)
    after_rows = shifted(grad_conv[:rim_size], "ctx", -1)
    grad_padded = jnp.concatenate([grad_conv, after_rows], axis=0)
    grad_product = tap_sum(grad_padded, mr_taps, row_count, True)
    grad_key_mr = grad_product * value_mr.astype(jnp.float32)
    grad_value_mr = grad_product * key_mr.astype(jnp.float32)
    tap_partial = tap_gradient(grad_conv, padded, mr_taps.shape[0])
    grad_taps = lax.psum(tap_partial, "ctx") * grad_scale
    columns = full_cot
    grad_weight = (
        lax.psum_scatter(
            lax.dot_general(
                columns, mixed_li, (((0,), (0,)), ((), ())), preferred_element_type=jnp.float32
            ),
            "ctx",
            scatter_dimension=0,
            tiled=True,
        )
        * grad_scale
    )
    return (
        output,
        grad_query_mr,
        grad_key_mr,
        grad_value_mr,
        grad_query_li,
        grad_key_li,
        grad_taps,
        grad_weight,
    )


def solution(mesh):
    return jax.shard_map(
        shards,
        mesh=mesh,
        in_specs=(
            P("ctx", "fsdp"),
            P("ctx", "fsdp"),
            P("ctx", "fsdp"),
            P("ctx", "fsdp"),
            P("ctx", "fsdp"),
            P(None, "fsdp"),
            P(None, "fsdp"),
            P(None, "fsdp"),
            P("fsdp"),
            P("ctx", "fsdp"),
            P("ctx", "fsdp"),
        ),
        out_specs=(
            P("ctx", "fsdp"),
            P("ctx", "fsdp"),
            P("ctx", "fsdp"),
            P("ctx", "fsdp"),
            P("ctx", "fsdp"),
            P("ctx", "fsdp"),
            P(None, "fsdp"),
            P("ctx", "fsdp"),
        ),
        check_vma=False,
    )
```

profile of v0, /device:TPU:1, one launch (start us, length us, event | category | flops | bytes accessed | tf_op | source)
XLA Modules:
  0.0 591.5 jit_solution(5253614610020019921)
XLA Ops:
  8.3 4.6 collective-permute-start
  12.9 1.4 broadcast_divide_fusion
  14.9 24.7 %while.127 = (s32[]{:T(128)}, f32[128,512]{1,0:T(8,128)S(1)}, f32[128,512]{1,0:T(8,128)}, bf16[255,512]{1,0:T(8,128)(2,1)S(1)}, s32[]{:T(128)}, /*index=5*/s32[]...) while((s32[]{:T(128)}, f32[128,512]{1,0:T(8,128)S(1)}, ...), condition=%wide.region_1.2_spmd.clone, body=%wide.region_0.1_spmd.clone.sunk | while | flops 1638467 | bytes 1623039 | solution.py:51
  42.6 22.2 %all-gather.13.cloned.1.call-done = f32[512,512]{1,0:T(8,128)} async-done(((f32[16,512]{1,0:T(8,128)}), f32[512,512]{1,0:T(8,128)}) %all-gather.13.cloned.1.call-update) | async-done | bytes 1048592 | tf_op jit(solution)/shard_map/all_gather | solution.py:17
  64.9 50.3 %all-gather.15.cloned.1.call-done = f32[512,512]{1,0:T(8,128)} async-done(((f32[16,512]{1,0:T(8,128)}), f32[512,512]{1,0:T(8,128)}) %all-gather.15.cloned.1.call-update) | async-done | bytes 1048592 | tf_op jit(solution)/shard_map/all_gather | solution.py:17
  115.2 26.0 %while.129 = (s32[]{:T(128)}, f32[16,512]{1,0:T(8,128)S(1)}, s32[]{:T(128)}, f32[32,16,512]{2,1,0:T(8,128)}, f32[32,16,512]{2,1,0:T(8,128)}, /*index=5*/s32[]{:T(128)}, s32[]{:T(128)}) while((s32[]{:T(128)}, f32[16,512]{1,0:T(8,128)S(1)}, s32[]{:T(128)}, f32[32,16,512]{2,1,0:T(8,128)}, f32[32,16,512]{2,1,0:T(8,128)}, ...), condition=%wide.region_5.6_spmd.clone, body=%wide.region_4.5_spmd.clone.sunk | while | flops 32772 | bytes 131181 | solution.py:28
  141.2 12.0 %while.133 = (s32[]{:T(128)}, f32[16,512]{1,0:T(8,128)S(1)}, f32[2,64,512]{2,1,0:T(8,128)S(1)}, f32[2,64,512]{2,1,0:T(8,128)S(1)}, f32[16,512]{1,0:T(8,128)S(1)}...) while((s32[]{:T(128)}, f32[16,512]{1,0:T(8,128)S(1)}, ...), condition=%wide.region_8.9_spmd.clone.clone, body=%wide.region_6.8_spmd.clone.clone.sunk | while | flops 407347200 | bytes 19857772 | solution.py:106
  142.8 2.1 fusion.77
  148.8 2.1 fusion.77
  153.3 53.7 %all-gather.9.cloned.1.call-done = bf16[4096,512]{1,0:T(8,128)(2,1)} async-done(((bf16[128,512]{1,0:T(8,128)(2,1)}), bf16[4096,512]{1,0:T(8,128)(2,1)}) %all-gather.9.cloned.1.call-update) | async-done | bytes 4194320 | tf_op jit(solution)/shard_map/all_gather | solution.py:152
  207.0 3.9 fusion.48
  212.9 47.2 %all-gather.17.cloned.1.call-done = f32[512,512]{1,0:T(8,128)} async-done(((f32[16,512]{1,0:T(8,128)}), f32[512,512]{1,0:T(8,128)}) %all-gather.17.cloned.1.call-update) | async-done | bytes 1048592 | tf_op jit(solution)/shard_map/all_gather | solution.py:17
  260.1 26.1 %while.131 = (s32[]{:T(128)}, f32[16,512]{1,0:T(8,128)S(1)}, s32[]{:T(128)}, f32[32,16,512]{2,1,0:T(8,128)}, f32[32,16,512]{2,1,0:T(8,128)}, /*index=5*/s32[]{:T(128)}, s32[]{:T(128)}, s32[]{:T(128)}, s32[]{:T(128)}) while((s32[]{:T(128)}, f32[16,512]{1,0:T(8,128)S(1)}, s32[]{:T(128)}, f32[32,16,512]{2,1,0:T(8,128)}, ...), condition=%wide.region_13.14_spmd.clone, body=%wide.region_12.13_spmd.clone.sunk | while | flops 32776 | bytes 131243 | solution.py:28
  286.2 12.0 %while.134 = (s32[]{:T(128)}, f32[16,512]{1,0:T(8,128)S(1)}, f32[2,64,512]{2,1,0:T(8,128)S(1)}, f32[2,64,512]{2,1,0:T(8,128)S(1)}, f32[16,512]{1,0:T(8,128)S(1)}...) while((s32[]{:T(128)}, f32[16,512]{1,0:T(8,128)S(1)}, ...), condition=%wide.region_16.17_spmd.clone.clone, body=%wide.region_14.16_spmd.clone.clone.sunk | while | flops 407347200 | bytes 19857772 | solution.py:106
  287.8 2.1 fusion.80
  293.8 2.1 fusion.80
  300.0 28.1 %while.126 = (s32[]{:T(128)}, f32[16,8,512]{2,1,0:T(8,128)S(1)}, s32[16]{0:T(128)S(1)}, bf16[255,512]{1,0:T(8,128)(2,1)S(1)}, f32[128,512]{1,0:T(8,128)S(1)}, /*...) while((s32[]{:T(128)}, f32[16,8,512]{2,1,0:T(8,128)S(1)}, ...), condition=%wide.region_28.29_spmd, body=%wide.region_19.28_spmd.sunk | while | flops 1568810 | bytes 1393317 | solution.py:70
  329.0 4.5 convolution_bitcast_fusion
  333.6 2.1 collective-permute-start.1
  335.7 5.0 fusion.52
  340.7 98.6 %all-reduce.2.cloned.1.call-done = f32[128,512]{0,1:T(8,128)} async-done(((f32[128,512]{0,1:T(8,128)}), f32[128,512]{0,1:T(8,128)}) %all-reduce.2.cloned.1.call-update) | async-done | bytes 262160 | tf_op jit(solution)/shard_map/psum | solution.py:189
  441.2 23.6 %while.132 = (s32[]{:T(128)}, f32[128,512]{1,0:T(8,128)S(1)}, f32[128,512]{1,0:T(8,128)}, f32[255,512]{1,0:T(8,128)S(1)}, s32[]{:T(128)}, /*index=5*/s32[]{:T(12...) while((s32[]{:T(128)}, f32[128,512]{1,0:T(8,128)S(1)}, ...), condition=%wide.region_18.19_spmd.clone, body=%wide.region_17.18_spmd.clone.sunk | while | flops 1114163 | bytes 2671495 | solution.py:51
  465.7 76.7 %reduce-scatter.5.cloned.1.call-done = f32[128,512]{0,1:T(8,128)} async-done(((f32[4096,512]{0,1:T(8,128)}), f32[128,512]{0,1:T(8,128)}) %reduce-scatter.5.cloned.1.call-update) | async-done | bytes 262160 | tf_op jit(solution)/shard_map/reduce_scatter | solution.py:192
  544.3 40.4 %reduce-scatter.3.cloned.1.call-done = f32[128,512]{1,0:T(8,128)} async-done(((f32[128,4096]{1,0:T(8,128)}), f32[128,512]{1,0:T(8,128)}) %reduce-scatter.3.cloned.1.call-update) | async-done | bytes 262160 | tf_op jit(solution)/shard_map/reduce_scatter | solution.py:156
  (298 shorter events, 142.6 us)
Async XLA Ops:
  7.2 57.7 %all-gather.13.cloned.1.call-start = ((), (), s32[]{:S(2)}) async-start(), calls=%async_computation.7 | async-start | bytes 1081344 | tf_op jit(solution)/shard_map/all_gather | solution.py:17
  8.3 6.5 %collective-permute-start = (bf16[127,512]{1,0:T(8,128)(2,1)S(1)}, bf16[127,512]{1,0:T(8,128)(2,1)S(1)}, u32[]{:S(2)}, u32[]{:S(2)}) collective-permute-start(bf16[127,512]{1,0:T(8,128)(2,1)S(1)} %slice.20), channel_id=1, source_target_pairs={{0,8},{8,16},{16,24},{24,32},{32,40},{40,48},{48,56},{56,64},{64,7... | collective-permute-start | bytes 390152 | tf_op jit(solution)/shard_map/ppermute | solution.py:12
  14.3 100.9 %all-gather.15.cloned.1.call-start = ((), (), s32[]{:S(2)}) async-start(), calls=%async_computation.8 | async-start | bytes 1081344 | tf_op jit(solution)/shard_map/all_gather | solution.py:17
  14.8 24.7 %copy-start.1 = (bf16[128,512]{1,0:T(8,128)(2,1)S(1)}, bf16[128,512]{1,0:T(8,128)(2,1)}, u32[]{:S(2)}) copy-start(bf16[128,512]{1,0:T(8,128)(2,1)} %param.29) | copy-start | bytes 393220
  14.8 24.7 %copy-start.4 = (bf16[128,512]{1,0:T(8,128)(2,1)S(1)}, bf16[128,512]{1,0:T(8,128)(2,1)}, u32[]{:S(2)}) copy-start(bf16[128,512]{1,0:T(8,128)(2,1)} %param.33) | copy-start | bytes 393220
  40.6 0.6 copy-start.2
  41.2 112.0 %all-gather.11.cloned.1.call-start = ((), (), s32[]{:S(2)}) async-start(), calls=%async_computation.4 | async-start | bytes 1179648 | tf_op jit(solution)/shard_map/all_gather | solution.py:157
  42.0 165.0 %all-gather.9.cloned.1.call-start = ((), (), s32[]{:S(2)}) async-start(), calls=%async_computation.2 | async-start | bytes 4325376 | tf_op jit(solution)/shard_map/all_gather | solution.py:152
  42.6 217.5 %all-gather.17.cloned.1.call-start = ((), (), s32[]{:S(2)}) async-start(), calls=%async_computation.9 | async-start | bytes 1081344 | tf_op jit(solution)/shard_map/all_gather | solution.py:17
  141.2 65.8 %copy-start.7 = (bf16[128,512]{1,0:T(8,128)(2,1)S(1)}, bf16[128,512]{1,0:T(8,128)(2,1)}, u32[]{:S(2)}) copy-start(bf16[128,512]{1,0:T(8,128)(2,1)} %param.32) | copy-start | bytes 393220
  141.2 65.8 %copy-start.8 = (f32[512]{0:T(512)S(1)}, f32[512]{0:T(512)}, u32[]{:S(2)}) copy-start(f32[512]{0:T(512)} %param.37) | copy-start | bytes 6148
  212.0 0.6 copy-start.3
  212.7 226.7 %all-reduce.2.cloned.1.call-start = ((), (), s32[]{:S(2)}) async-start(), calls=%async_computation.5 | async-start | bytes 524288 | tf_op jit(solution)/shard_map/psum | solution.py:189
  300.0 29.0 %copy-start = (bf16[128,4096]{1,0:T(8,128)(2,1)S(1)}, bf16[128,4096]{1,0:T(8,128)(2,1)}, u32[]{:S(2)}) copy-start(bf16[128,4096]{1,0:T(8,128)(2,1)} %all-gather.11.cloned.1.call-done) | copy-start | bytes 3145732
  328.9 213.5 %reduce-scatter.5.cloned.1.call-start = ((), (), s32[]{:S(2)}) async-start(), calls=%async_computation.6 | async-start | bytes 8650752 | tf_op jit(solution)/shard_map/reduce_scatter | solution.py:192
  333.5 251.1 %reduce-scatter.3.cloned.1.call-start = ((), (), s32[]{:S(2)}) async-start(), calls=%async_computation.3 | async-start | bytes 2359296 | tf_op jit(solution)/shard_map/reduce_scatter | solution.py:156
  333.6 107.6 %collective-permute-start.1 = (f32[127,512]{1,0:T(8,128)S(1)}, f32[127,512]{1,0:T(8,128)S(1)}, u32[]{:S(2)}, u32[]{:S(2)}) collective-permute-start(f32[127,512]{1,0:T(8,128)S(1)} %bitcast.266), channel_id=1, source_target_pairs={{8,0},{16,8},{24,16},{32,24},{40,32},{48,40},{56,48},{64,56},{72,6... | collective-permute-start | bytes 780296 | tf_op jit(solution)/shard_map/ppermute | solution.py:12
  441.2 23.6 %copy-start.5 = (bf16[128,512]{1,0:T(8,128)(2,1)S(1)}, bf16[128,512]{1,0:T(8,128)(2,1)}, u32[]{:S(2)}) copy-start(bf16[128,512]{1,0:T(8,128)(2,1)} %param.31) | copy-start | bytes 393220
  441.2 23.6 %copy-start.6 = (bf16[128,512]{1,0:T(8,128)(2,1)S(1)}, bf16[128,512]{1,0:T(8,128)(2,1)}, u32[]{:S(2)}) copy-start(bf16[128,512]{1,0:T(8,128)(2,1)} %param.30) | copy-start | bytes 393220
Sparse Core Ops, SparseCore 0:
  14.4 50.3 all-gather.12
  68.0 47.1 all-gather.14
  117.0 32.5 all-gather.10
  152.0 54.9 all-gather.8
  212.8 47.2 all-gather.16
  329.0 110.2 all-reduce.1
  443.9 98.4 reduce-scatter.4
  545.6 39.0 reduce-scatter.2
where the time goes:
time: 602 us; the launch traced here: 591 us
  waiting for transfers between devices  391 us (65%)
  other arithmetic  82.4 us (14%)
  local copies, waits for them, and re-layouts  57.5 us (10%)
  matrix products  21.8 us (4%)
  loops' own time  17.2 us (3%)
  between operations  14.5 us (2%)
  starting transfers between devices  7.24 us (1%)
    all_gather x3, waiting for transfers between devices, entering(): everything = jax.tree.map(lambda part: lax.all_gather(part, axis), x)  120 us
    psum x1, waiting for transfers between devices, shards(): grad_taps = lax.psum(tap_partial, 'ctx') * grad_scale  98.6 us
    reduce_scatter x1, waiting for transfers between devices, shards(): lax.psum_scatter(lax.dot_general(columns, mixed_li, (((0,), (0,)), ((), (...  76.7 us
    all_gather x1, waiting for transfers between devices, shards(): lax.all_gather(out_weight, 'ctx', axis=0, tiled=True)  53.7 us
    select_n x64, other arithmetic, lap(): return jax.tree.map(lambda a, b: jnp.where(reached, a, b), new, before)  50.5 us
    reduce_scatter x1, waiting for transfers between devices, shards(): lax.psum_scatter(partial_out, 'fsdp', scatter_dimension=1, tiled=True)  40.4 us
    dynamic_slice x32, local copies, waits for them, and re-layouts, one_turn(): lax.dynamic_index_in_dim(tap_weights, tap_index, 0, keepdims=False)  33.3 us
  transfers between devices with their start and end apart: 10, of which 8 were waited for; matrix products, arithmetic and copies ran while one was open for 17% of the time, Pallas kernels for 0%

commit v1 on v0

v1 whole, which is shorter than its diff:
```python
import functools
import math

import jax
import jax.numpy as jnp
import ml_dtypes
import numpy as np
from jax import lax
from jax.experimental import pallas as pl
from jax.experimental.pallas import tpu as pltpu
from jax.sharding import PartitionSpec as P

BF = jnp.bfloat16
F32 = jnp.float32
MESH = pl.DeviceIdType.MESH
ROWS = 128
COLS = 512
MODES = 16
RING = 4
CHIPS = RING * RING
LANES = 128
GROUPS = COLS // LANES


def split_const(m):
    hi = m.astype(ml_dtypes.bfloat16)
    lo = (m - hi.astype(np.float64)).astype(ml_dtypes.bfloat16)
    return hi, lo


def transforms():
    theta = 2.0 * np.pi * (np.arange(ROWS) + 0.5)[:, None] / (2 * ROWS)

    def forward(places):
        return np.concatenate([np.cos(theta * places), -np.sin(theta * places)], axis=0)

    here = forward(np.arange(ROWS)[None, :].astype(np.float64))
    past = forward(np.arange(-ROWS, 0)[None, :].astype(np.float64))
    here_hi, here_lo = split_const(here)
    past_hi, past_lo = split_const(past)
    back_hi, back_lo = split_const(here.T / ROWS)
    return (
        np.concatenate([here_hi, here_hi, here_lo], axis=1),
        np.concatenate([past_hi, past_lo], axis=1),
        np.concatenate([back_hi, back_hi, back_lo], axis=1),
    )


def dot(a, b):
    return jnp.dot(a, b, preferred_element_type=F32)


def split3(v):
    hi = v.astype(BF)
    lo = (v - hi.astype(F32)).astype(BF)
    return jnp.concatenate([hi, lo, hi], axis=0)


def times(a, b):
    ar, ai, br, bi = a[:ROWS], a[ROWS:], b[:ROWS], b[ROWS:]
    return jnp.concatenate([ar * br - ai * bi, ar * bi + ai * br], axis=0)


def conj_times(a, b):
    ar, ai, br, bi = a[:ROWS], a[ROWS:], b[:ROWS], b[ROWS:]
    return jnp.concatenate([ar * br + ai * bi, ar * bi - ai * br], axis=0)


ID_A1 = 0
ID_A2 = 4
ID_C = 20
ID_HALO = 38
ID_BACK_HALO = 39
ID_SF1 = 40
ID_SF3 = 41
ID_SB1 = 42
ID_SB3 = 43
ID_MIX = 44
ID_GM = 45
ID_OUT = 46
ID_T1 = 47
ID_T4 = 48
ID_SF2 = 49
ID_SB2 = 65
ID_D = 81
ID_T2 = 97
ID_T3 = 113
ID_B = 129
ID_COUNT = 140

SCRATCH = dict(
    product=((ROWS, COLS), BF),
    prev=((ROWS, COLS), BF),
    grad_halo=((ROWS, COLS), BF),
    after=((ROWS, COLS), BF),
    wg=((CHIPS, ROWS, COLS), BF),
    cg=((8, 2 * ROWS, 256), BF),
    mixed=((2 * ROWS, COLS), BF),
    mixed_mr=((ROWS, COLS), BF),
    tap_spec=((2 * ROWS, COLS), F32),
    long_spec=((2 * ROWS, COLS), F32),
    prod_spec=((2 * ROWS, COLS), F32),
    mr_conv=((ROWS, COLS), F32),
    signal=((ROWS, COLS), F32),
    li_out=((ROWS, COLS), F32),
    work=((ROWS, COLS), F32),
    d8=((MODES, 8, COLS), F32),
    up0=((MODES, 8, COLS), F32),
    up7=((MODES, 8, COLS), F32),
    c0=((MODES, 8, COLS), F32),
    c1=((MODES, 8, COLS), F32),
    c8=((MODES, 8, COLS), F32),
    dev_decay=((MODES, COLS), F32),
    chip_decay=((MODES, COLS), F32),
    f_own=((MODES, COLS), F32),
    f_mate=((MODES, COLS), F32),
    f_chip=((8, COLS), F32),
    f_slots=((CHIPS, 8, COLS), F32),
    f_in=((MODES, COLS), F32),
    b_own=((MODES, COLS), F32),
    b_mate=((MODES, COLS), F32),
    b_chip=((8, COLS), F32),
    b_slots=((CHIPS, 8, COLS), F32),
    b_in=((MODES, COLS), F32),
    enter=((MODES, COLS), F32),
    gm_part=((2 * ROWS, COLS), F32),
    gm_mate=((ROWS, COLS), F32),
    spec=((2 * ROWS, COLS), F32),
    grad_out=((ROWS, COLS), F32),
    dw_send=((CHIPS, ROWS, COLS), BF),
    dw_slots=((CHIPS, ROWS, COLS), BF),
    o_send=((8, 2 * ROWS, 256), BF),
    o_slots=((8, 2 * ROWS, 256), BF),
    o_sum=((2 * ROWS, 256), F32),
    o_mate=((ROWS, 256), F32),
    t_own=((ROWS, COLS), F32),
    t_mate=((ROWS // 2, COLS), F32),
    t_half=((ROWS // 2, COLS), F32),
    t_slots=((CHIPS, 8, 256), F32),
    t_done=((8, 256), F32),
    t_all=((ROWS, COLS), F32),
    out=((ROWS, COLS), F32),
    gqm=((ROWS, COLS), F32),
    gkm=((ROWS, COLS), F32),
    gvm=((ROWS, COLS), F32),
    gql=((ROWS, COLS), F32),
    gkl=((ROWS, COLS), F32),
    gw=((ROWS, COLS), F32),
)


INPUTS = (
    ((ROWS, COLS), BF),
    ((ROWS, COLS), BF),
    ((ROWS, COLS), BF),
    ((ROWS, COLS), BF),
    ((ROWS, COLS), F32),
    ((MODES, COLS), F32),
    ((MODES, COLS), F32),
    ((ROWS, COLS), BF),
    ((ROWS, COLS), BF),
    ((ROWS, COLS), BF),
    ((1, COLS), F32),
    ((2 * ROWS, 3 * ROWS), BF),
    ((2 * ROWS, 2 * ROWS), BF),
    ((ROWS, 6 * ROWS), BF),
)


def kernel(*refs):
    n_in = len(INPUTS)
    given = refs[:n_in]
    results = refs[n_in : n_in + 8]
    held = refs[n_in + 8 : n_in + 8 + n_in]
    (km, vm, cot, w, taps, time, residue, qm, kl, ql, skip, fwd3, past2, inv3) = held
    s = dict(zip(SCRATCH, refs[2 * n_in + 8 :]))
    out, gqm, gkm, gvm, gql, gkl, gw = (s[n] for n in ("out", "gqm", "gkm", "gvm", "gql", "gkl", "gw"))
    snd, rcv, ld, st = refs[2 * n_in + 8 + len(SCRATCH) :]

    def load(i):
        return pltpu.make_async_copy(given[i], held[i], ld.at[i])

    for i in range(n_in):
        load(i).start()

    stored = []

    def store(source, i):
        c = pltpu.make_async_copy(source, results[i], st.at[i])
        c.start()
        stored.append(c)

    n_z = 8
    grad_scale = 1.0 / math.sqrt(ROWS * 2 * CHIPS)
    me = lax.axis_index("ctx")
    z = lax.axis_index("fsdp")
    k = lax.rem(me, 2)
    chip = lax.div(me, 2)
    x, y = lax.div(chip, RING), lax.rem(chip, RING)
    a = x * (1 - k) + y * k
    b = y * (1 - k) + x * k

    def ring(v, by):
        return lax.rem(v + by + RING, RING)

    def at(pa, pb):
        return (pa * RING + pb) * (1 - k) + (pb * RING + pa) * k

    def plane(c, core):
        return (c * 2 + core, z)

    mate = (chip * 2 + (1 - k), z)

    def up(dz):
        return (me, lax.rem(z + dz + n_z, n_z))

    def copy(src, dst, i, to):
        return pltpu.make_async_remote_copy(
            src_ref=src, dst_ref=dst, send_sem=snd.at[i], recv_sem=rcv.at[i], device_id=to, device_id_type=MESH
        )

    pending = []

    def send(src, dst, i, to):
        c = copy(src, dst, i, to)
        c.start()
        pending.append(c)

    def arrived(dst, i, to):
        copy(dst, dst, i, to).wait_recv()

    def half(h):
        return pl.ds(pl.multiple_of(h * ROWS, ROWS), ROWS)

    def chip_off(by):
        return lax.rem(chip + by + CHIPS, CHIPS)

    barrier = pltpu.get_barrier_semaphore()
    pl.semaphore_signal(barrier, inc=1, device_id=mate, device_id_type=MESH)

    def greet_chip(d, carry):
        pl.semaphore_signal(barrier, inc=1, device_id=plane(chip_off(d), k), device_id_type=MESH)
        return carry

    lax.fori_loop(1, CHIPS, greet_chip, 0)

    def greet_z(d, carry):
        pl.semaphore_signal(barrier, inc=1, device_id=up(d), device_id_type=MESH)
        return carry

    lax.fori_loop(1, n_z, greet_z, 0)
    last = 2 * CHIPS - 1
    across = (me + 2 * k - 1, z)

    @pl.when((me > 0) & (me < last))
    def _():
        pl.semaphore_signal(barrier, inc=1, device_id=across, device_id_type=MESH)

    for i in range(4):
        load(i).wait()
    s["product"][...] = (km[...].astype(F32) * vm[...].astype(F32)).astype(BF)
    for h in range(2):
        s["cg"][z, half(k), h * LANES : (h + 1) * LANES] = cot[
            :, pl.ds(pl.multiple_of((2 * h + k) * LANES, LANES), LANES)
        ]
    s["wg"][chip] = w[...]

    peers = 1 + (CHIPS - 1) + (n_z - 1)

    @pl.when((me == 0) | (me == last))
    def _():
        pl.semaphore_wait(barrier, peers)

    @pl.when((me > 0) & (me < last))
    def _():
        pl.semaphore_wait(barrier, peers + 1)

    nxt = (lax.rem(me + 1, last + 1), z)
    prv = (lax.rem(me + last, last + 1), z)

    halo = copy(s["product"], s["prev"], ID_HALO, nxt)

    @pl.when(me < last)
    def _():
        halo.start()

    a_next, a_prev = plane(at(ring(a, 1), b), k), plane(at(ring(a, -1), b), k)
    b_next, b_prev = plane(at(a, ring(b, 1)), k), plane(at(a, ring(b, -1)), k)
    low, high = pl.ds(0, ROWS // 2), pl.ds(ROWS // 2, ROWS // 2)
    wg = s["wg"]

    def wblock(ra, rb):
        return wg.at[at(ring(a, ra), ring(b, rb))]

    def whalf(ra, rb, rows):
        return wg.at[at(ring(a, ra), ring(b, rb)), rows]

    REL = (0, -1, 1, 2)

    def a2_send(j):
        block = wblock(REL[j], 0)
        send(block, block, ID_A2 + 4 * j, b_next)
        send(block, block, ID_A2 + 4 * j + 1, b_prev)

    def a1_send():
        block = wblock(0, 0)
        send(block, block, ID_A1, a_next)
        send(block, block, ID_A1 + 1, a_prev)

    def a1_forward():
        arrived(wblock(-1, 0), ID_A1, a_next)
        send(whalf(-1, 0, low), whalf(-1, 0, low), ID_A1 + 2, a_next)
        a2_send(1)
        arrived(wblock(1, 0), ID_A1 + 1, a_prev)
        send(whalf(1, 0, high), whalf(1, 0, high), ID_A1 + 3, a_prev)
        a2_send(2)

    def a1_finish():
        arrived(whalf(2, 0, low), ID_A1 + 2, a_next)
        arrived(whalf(2, 0, high), ID_A1 + 3, a_prev)
        a2_send(3)

    def a2_forward(j):
        ra = REL[j]
        arrived(wblock(ra, -1), ID_A2 + 4 * j, b_next)
        send(whalf(ra, -1, low), whalf(ra, -1, low), ID_A2 + 4 * j + 2, b_next)
        arrived(wblock(ra, 1), ID_A2 + 4 * j + 1, b_prev)
        send(whalf(ra, 1, high), whalf(ra, 1, high), ID_A2 + 4 * j + 3, b_prev)

    def a2_finish(j):
        ra = REL[j]
        arrived(whalf(ra, 2, low), ID_A2 + 4 * j + 2, b_next)
        arrived(whalf(ra, 2, high), ID_A2 + 4 * j + 3, b_prev)

    cg = s["cg"]
    z_next, z_prev = up(1), up(-1)

    def cblock(rz, chunk):
        rows = half(k) if chunk == 0 else half(1 - k)
        return cg.at[lax.rem(z + rz + n_z, n_z), rows]

    def c_id(direction, step, chunk):
        return ID_C + 2 + direction * 8 + (step - 1) * 2 + chunk

    def c_mate_refs(h, core):
        return cg.at[z, half(k if core else 1 - k), pl.ds(h * LANES, LANES)]

    def c_start():
        for h in range(2):
            send(
                cot.at[:, pl.ds(pl.multiple_of((2 * h + 1 - k) * LANES, LANES), LANES)],
                c_mate_refs(h, True),
                ID_C + h,
                mate,
            )
        send(cblock(0, 0), cblock(0, 0), c_id(0, 1, 0), z_next)
        send(cblock(0, 0), cblock(0, 0), c_id(1, 1, 0), z_prev)

    def c_second():
        for h in range(2):
            arrived(c_mate_refs(h, False), ID_C + h, mate)
        send(cblock(0, 1), cblock(0, 1), c_id(0, 1, 1), z_next)
        send(cblock(0, 1), cblock(0, 1), c_id(1, 1, 1), z_prev)

    def c_forward(step, chunk):
        arrived(cblock(-step, chunk), c_id(0, step, chunk), z_next)
        if step < 3 or chunk == 0:
            send(cblock(-step, chunk), cblock(-step, chunk), c_id(0, step + 1, chunk), z_next)
        arrived(cblock(step, chunk), c_id(1, step, chunk), z_prev)
        if step < 3 or chunk == 1:
            send(cblock(step, chunk), cblock(step, chunk), c_id(1, step + 1, chunk), z_prev)

    def c_finish():
        arrived(cblock(-4, 0), c_id(0, 4, 0), z_next)
        arrived(cblock(4, 1), c_id(1, 4, 1), z_prev)

    a1_send()
    c_start()
    a2_send(0)

    for i in range(4, n_in):
        load(i).wait()

    within = lax.broadcasted_iota(jnp.int32, (1, 8, LANES), 1).astype(F32)

    def tables(g, carry):
        lanes = pl.ds(pl.multiple_of(g * LANES, LANES), LANES)
        rate = 1.0 / time[:, lanes]
        u = 2.0 * rate
        series = 1.0 - u * (1.0 / 7.0)
        for n in (6, 5, 4, 3, 2):
            series = 1.0 - u * (1.0 / n) * series
        coef = residue[:, lanes] * jnp.sqrt(u * series)
        s["dev_decay"][:, lanes] = jnp.exp(-rate * ROWS)
        s["chip_decay"][:, lanes] = jnp.exp(-rate * (2 * ROWS))
        r3 = jnp.broadcast_to(rate[:, None, :], (MODES, 8, LANES))
        c3 = jnp.broadcast_to(coef[:, None, :], (MODES, 8, LANES))
        s["d8"][:, :, lanes] = jnp.exp(-r3 * 8.0)
        up0 = jnp.exp(-r3 * within)
        s["up0"][:, :, lanes] = up0
        s["up7"][:, :, lanes] = jnp.exp(-r3 * (7.0 - within))
        s["c0"][:, :, lanes] = c3 * up0
        s["c1"][:, :, lanes] = c3 * jnp.exp(-r3 * (within + 1.0))
        s["c8"][:, :, lanes] = c3 * jnp.exp(-r3 * (8.0 - within))
        return carry

    lax.fori_loop(0, GROUPS, tables, 0)

    def spread(table, state, target, descending):
        def one(g, carry):
            lanes = pl.ds(pl.multiple_of(g * LANES, LANES), LANES)
            d8 = s["d8"][:, :, lanes]
            v = table[:, :, lanes]
            if state is not None:
                v = v * jnp.broadcast_to(state[:, lanes][:, None, :], (MODES, 8, LANES))
            for t in range(ROWS // 8):
                tile = ROWS // 8 - 1 - t if descending else t
                target[tile * 8 : tile * 8 + 8, lanes] = jnp.sum(v, axis=0)
                if t < ROWS // 8 - 1:
                    v = v * d8
            return carry

        lax.fori_loop(0, GROUPS, one, 0)

    def gather_state(source, table, target, descending):
        def one(g, carry):
            lanes = pl.ds(pl.multiple_of(g * LANES, LANES), LANES)
            d8 = s["d8"][:, :, lanes]
            v = jnp.zeros((MODES, 8, LANES), F32)
            for t in range(ROWS // 8):
                tile = ROWS // 8 - 1 - t if descending else t
                rows = source[tile * 8 : tile * 8 + 8, lanes][None]
                v = v * d8 + rows if t else v + rows
            target[:, lanes] = jnp.sum(v * table[:, :, lanes], axis=1)
            return carry

        lax.fori_loop(0, GROUPS, one, 0)

    def transform(v):
        return dot(fwd3[...], split3(v))

    def inverse(v):
        return dot(inv3[...], split3(v))

    c_second()
    s["tap_spec"][...] = transform(taps[...])
    a1_forward()
    spread(s["c0"], None, s["work"], False)
    c_forward(1, 0)
    s["long_spec"][...] = transform(s["work"][...])

    @pl.when(me > 0)
    def _():
        halo.wait_recv()

    @pl.when(me == 0)
    def _():
        s["prev"][...] = jnp.zeros((ROWS, COLS), BF)

    here2 = jnp.concatenate([fwd3[:, :ROWS], fwd3[:, 2 * ROWS :]], axis=1)
    p, q = s["product"][...], s["prev"][...]
    s["prod_spec"][...] = dot(here2, jnp.concatenate([p, p], axis=0)) + dot(
        past2[...], jnp.concatenate([q, q], axis=0)
    )
    a1_finish()
    s["mr_conv"][...] = inverse(times(s["prod_spec"][...], s["tap_spec"][...]))
    mixed_mr = (qm[...].astype(F32) * s["mr_conv"][...]).astype(BF)
    s["mixed_mr"][...] = mixed_mr
    s["signal"][...] = (kl[...].astype(F32) * mixed_mr.astype(F32)).astype(BF).astype(F32)

    own8 = pl.ds(pl.multiple_of(k * 8, 8), 8)

    def chip_state(own, theirs, into, slots, id2, id3, target, descending):
        decay = s["dev_decay"][own8, :]
        mine, other = own[own8, :], theirs[own8, :]
        near = jnp.where(k == 0, mine, other)
        far = jnp.where(k == 0, other, mine)
        into[...] = near + decay * far if descending else decay * near + far
        sign = -1 if descending else 1
        ahead = chip if descending else CHIPS - 1 - chip
        behind = CHIPS - 1 - chip if descending else chip

        def put(d, carry):
            @pl.when(d <= ahead)
            def _():
                copy(into, slots.at[d], id2 + d, plane(chip_off(sign * d), k)).start()

            return carry

        lax.fori_loop(1, CHIPS, put, 0)

    def chip_finish(into, slots, id2, id3, target, descending):
        sign = -1 if descending else 1
        ahead = chip if descending else CHIPS - 1 - chip
        behind = CHIPS - 1 - chip if descending else chip

        def take(d, carry):
            @pl.when(d <= behind)
            def _():
                copy(into, slots.at[d], id2 + d, plane(chip_off(sign * d), k)).wait_recv()

            return carry

        lax.fori_loop(1, CHIPS, take, 0)
        decay = s["chip_decay"][own8, :]
        total = jnp.zeros((8, COLS), F32)
        for d in range(CHIPS - 1, 0, -1):
            total = jnp.where(d <= behind, total * decay + slots[d], 0.0)
        target[own8, :] = total
        send(target.at[own8], target.at[own8], id3, mate)

        def sent(d, carry):
            @pl.when(d <= ahead)
            def _():
                copy(into, slots.at[d], id2 + d, plane(chip_off(sign * d), k)).wait_send()

            return carry

        return lambda: lax.fori_loop(1, CHIPS, sent, 0)

    other8 = pl.ds(pl.multiple_of((1 - k) * 8, 8), 8)

    gather_state(s["signal"], s["up7"], s["f_own"], False)
    send(s["f_own"], s["f_mate"], ID_SF1, mate)
    a2_forward(0)
    c_forward(1, 1)
    arrived(s["f_mate"], ID_SF1, mate)
    chip_state(s["f_own"], s["f_mate"], s["f_chip"], s["f_slots"], ID_SF2, ID_SF3, s["f_in"], False)
    a2_forward(1)
    spectrum = times(transform(s["signal"][...]), s["long_spec"][...])
    s["li_out"][...] = inverse(spectrum) + skip[...] * s["signal"][...]
    c_forward(2, 0)
    a2_forward(2)
    f_sent = chip_finish(s["f_chip"], s["f_slots"], ID_SF2, ID_SF3, s["f_in"], False)
    c_forward(2, 1)
    arrived(s["f_in"].at[other8], ID_SF3, mate)
    s["enter"][...] = jnp.where(
        k == 0, s["f_in"][...], s["dev_decay"][...] * s["f_in"][...] + s["f_mate"][...]
    )
    spread(s["c1"], s["enter"], s["work"], False)
    s["li_out"][...] = s["li_out"][...] + s["work"][...]
    s["mixed"][half(k), :] = (ql[...].astype(F32) * s["li_out"][...]).astype(BF)
    send(s["mixed"].at[half(k)], s["mixed"].at[half(k)], ID_MIX, mate)
    a2_forward(3)
    c_forward(3, 0)
    c_forward(3, 1)
    for j in range(4):
        a2_finish(j)
    c_finish()

    s["gm_part"][...] = jnp.zeros((2 * ROWS, COLS), F32)

    def contract(j, carry):
        block = wg[pl.ds(2 * j, 2)].reshape(2 * ROWS, COLS)
        s["gm_part"][...] += dot(cg[j], block)
        return carry

    lax.fori_loop(0, n_z, contract, 0)
    send(s["gm_part"].at[half(1 - k)], s["gm_mate"], ID_GM, mate)

    arrived(s["mixed"].at[half(1 - k)], ID_MIX, mate)

    def project(j, carry):
        part = lax.dot_general(
            cg[j], s["mixed"][...], (((0,), (0,)), ((), ())), preferred_element_type=F32
        ).astype(BF)
        s["dw_send"][2 * j] = part[:ROWS]
        s["dw_send"][2 * j + 1] = part[ROWS:]
        return carry

    lax.fori_loop(0, n_z, project, 0)

    def d_copy(d):
        to = chip_off(d)
        return copy(s["dw_send"].at[to], s["dw_slots"].at[d], ID_D + d, plane(to, k))

    def loop(first, count, action):
        def step(d, carry):
            action(d)
            return carry

        lax.fori_loop(first, count, step, 0)

    arrived(s["gm_mate"], ID_GM, mate)
    gm = s["gm_part"][half(k), :] + s["gm_mate"][...]
    gql[...] = gm * s["li_out"][...]
    store(gql, 4)
    s["grad_out"][...] = gm * ql[...].astype(F32)
    gather_state(s["grad_out"], s["up0"], s["b_own"], True)
    send(s["b_own"], s["b_mate"], ID_SB1, mate)
    spectrum = conj_times(s["long_spec"][...], transform(s["grad_out"][...]))
    arrived(s["b_mate"], ID_SB1, mate)
    chip_state(s["b_own"], s["b_mate"], s["b_chip"], s["b_slots"], ID_SB2, ID_SB3, s["b_in"], True)
    loop(1, CHIPS, lambda d: d_copy(d).start())
    s["grad_out"][...] = inverse(spectrum) + skip[...] * s["grad_out"][...]

    def o_copy(dz):
        return copy(s["o_send"].at[dz], s["o_slots"].at[dz], ID_B + dz, up(dz))

    def share(dz, carry):
        j = lax.rem(z + dz, n_z)
        block = wg[pl.ds(2 * j, 2)].reshape(2 * ROWS, COLS)
        s["o_send"][dz] = lax.dot_general(
            s["mixed"][...], block, (((1,), (1,)), ((), ())), preferred_element_type=F32
        ).astype(BF)
        o_copy(dz).start()
        return carry

    lax.fori_loop(1, n_z, share, 0)
    s["o_sum"][...] = lax.dot_general(
        s["mixed"][...],
        wg[pl.ds(2 * z, 2)].reshape(2 * ROWS, COLS),
        (((1,), (1,)), ((), ())),
        preferred_element_type=F32,
    )

    b_sent = chip_finish(s["b_chip"], s["b_slots"], ID_SB2, ID_SB3, s["b_in"], True)
    arrived(s["b_in"].at[other8], ID_SB3, mate)
    s["enter"][...] = jnp.where(
        k == 1, s["b_in"][...], s["dev_decay"][...] * s["b_in"][...] + s["b_mate"][...]
    )
    spread(s["c8"], s["enter"], s["work"], True)
    gli = s["grad_out"][...] + s["work"][...]
    gkl[...] = gli * s["mixed_mr"][...].astype(F32)
    gmm = gli * kl[...].astype(F32)
    gqm[...] = gmm * s["mr_conv"][...]
    gconv = gmm * qm[...].astype(F32)
    s["work"][...] = gconv
    s["grad_halo"][...] = gconv.astype(BF)
    back = copy(s["grad_halo"], s["after"], ID_BACK_HALO, prv)

    @pl.when(me > 0)
    def _():
        back.start()

    store(gkl, 5)
    store(gqm, 1)

    spec = transform(s["work"][...])
    s["spec"][...] = spec
    s["t_own"][...] = inverse(conj_times(s["prod_spec"][...], spec))
    th = ROWS // 2

    def trows(core):
        return pl.ds(pl.multiple_of(core * th, th), th)

    send(s["t_own"].at[trows(1 - k)], s["t_mate"], ID_T1, mate)

    @pl.when(me == last)
    def _():
        s["after"][...] = jnp.zeros((ROWS, COLS), BF)

    @pl.when(me < last)
    def _():
        back.wait_recv()

    arrived(s["t_mate"], ID_T1, mate)
    s["t_half"][...] = s["t_own"][trows(k), :] + s["t_mate"][...]

    def piece(c, base):
        rows = pl.ds(pl.multiple_of(base + lax.div(c, 2) * 8, 8), 8)
        lanes = pl.ds(pl.multiple_of(lax.rem(c, 2) * 256, 256), 256)
        return rows, lanes

    def t2_copy(d):
        to = chip_off(d)
        rows, lanes = piece(to, 0)
        return copy(s["t_half"].at[rows, lanes], s["t_slots"].at[d], ID_T2 + d, plane(to, k))

    loop(1, CHIPS, lambda d: t2_copy(d).start())

    n = s["after"][...]
    spec = s["spec"][...] - dot(past2[...], jnp.concatenate([n, n], axis=0))
    gp = inverse(conj_times(s["tap_spec"][...], spec))
    gkm[...] = gp * vm[...].astype(F32)
    gvm[...] = gp * km[...].astype(F32)
    store(gkm, 2)
    store(gvm, 3)

    loop(1, CHIPS, lambda d: t2_copy(d).wait_recv())
    rows, lanes = piece(chip, 0)
    total = s["t_half"][rows, lanes]
    for d in range(1, CHIPS):
        total = total + s["t_slots"][d]
    total = total * grad_scale
    s["t_done"][...] = total
    rows, lanes = piece(chip, k * th)
    s["t_all"][rows, lanes] = total

    def t3_copy(d):
        return copy(s["t_done"], s["t_all"].at[rows, lanes], ID_T3 + d, plane(chip_off(d), k))

    def t3_arrived(d):
        rows_from, lanes_from = piece(chip_off(-d), k * th)
        copy(s["t_done"], s["t_all"].at[rows_from, lanes_from], ID_T3 + d, plane(chip_off(d), k)).wait_recv()

    loop(1, CHIPS, lambda d: t3_copy(d).start())

    loop(1, n_z, lambda d: o_copy(d).wait_recv())
    total = s["o_sum"][...]
    for d in range(1, n_z):
        total = total + s["o_slots"][d].astype(F32)
    s["o_sum"][...] = total
    send(s["o_sum"].at[half(1 - k)], s["o_mate"], ID_OUT, mate)

    loop(1, CHIPS, t3_arrived)
    send(s["t_all"].at[trows(k)], s["t_all"].at[trows(k)], ID_T4, mate)

    loop(1, CHIPS, lambda d: d_copy(d).wait_recv())
    total = s["dw_send"][chip].astype(F32)
    for d in range(1, CHIPS):
        total = total + s["dw_slots"][d].astype(F32)
    gw[...] = total * grad_scale
    store(gw, 7)

    arrived(s["o_mate"], ID_OUT, mate)
    for h in range(2):
        mine = pl.ds(pl.multiple_of((2 * h + k) * LANES, LANES), LANES)
        theirs = pl.ds(pl.multiple_of((2 * h + 1 - k) * LANES, LANES), LANES)
        out[:, mine] = s["o_sum"][half(k), h * LANES : (h + 1) * LANES]
        out[:, theirs] = s["o_mate"][:, h * LANES : (h + 1) * LANES]
    store(out, 0)

    arrived(s["t_all"].at[trows(1 - k)], ID_T4, mate)
    store(s["t_all"], 6)

    for c in stored:
        c.wait()
    for c in pending:
        c.wait_send()
    f_sent()
    b_sent()
    loop(1, CHIPS, lambda d: d_copy(d).wait_send())
    loop(1, CHIPS, lambda d: t2_copy(d).wait_send())
    loop(1, CHIPS, lambda d: t3_copy(d).wait_send())
    loop(1, n_z, lambda d: o_copy(d).wait_send())

    @pl.when(me < last)
    def _():
        halo.wait_send()

    @pl.when(me > 0)
    def _():
        back.wait_send()


def shards(query_mr, key_mr, value_mr, query_li, key_li, mr_taps, li_time, li_residue, li_skip, out_weight, cotangent):
    consts = [jnp.asarray(m) for m in transforms()]
    args = (
        key_mr,
        value_mr,
        cotangent,
        out_weight,
        mr_taps,
        li_time,
        li_residue,
        query_mr,
        key_li,
        query_li,
        li_skip.reshape(1, COLS),
        *consts,
    )
    block = jax.ShapeDtypeStruct((ROWS, COLS), F32)
    hbm = pl.BlockSpec(memory_space=pltpu.HBM)
    results = pl.pallas_call(
        kernel,
        out_shape=(block,) * 8,
        in_specs=[hbm] * len(args),
        out_specs=(hbm,) * 8,
        scratch_shapes=[pltpu.VMEM(shape, kind) for shape, kind in INPUTS + tuple(SCRATCH.values())]
        + [pltpu.SemaphoreType.DMA((ID_COUNT,)), pltpu.SemaphoreType.DMA((ID_COUNT,)), pltpu.SemaphoreType.DMA((len(INPUTS),)), pltpu.SemaphoreType.DMA((8,))],
        compiler_params=pltpu.CompilerParams(
            collective_id=0, has_side_effects=True, vmem_limit_bytes=60 * 1024 * 1024
        ),
        cost_estimate=pl.CostEstimate(flops=3_000_000_000, bytes_accessed=4_000_000, transcendentals=1_000_000),
    )(*args)
    return pl.pallas_call(
        write_out,
        out_shape=(block,) * 8,
        in_specs=[hbm] * 8,
        out_specs=(hbm,) * 8,
        scratch_shapes=[pltpu.SemaphoreType.DMA((8,))],
        compiler_params=pltpu.CompilerParams(vmem_limit_bytes=60 * 1024 * 1024),
        cost_estimate=pl.CostEstimate(flops=0, bytes_accessed=4_000_000, transcendentals=0),
    )(*results)


def write_out(*refs):
    copies = [pltpu.make_async_copy(refs[i], refs[8 + i], refs[16].at[i]) for i in range(8)]
    for c in copies:
        c.start()
    for c in copies:
        c.wait()


def solution(mesh):
    rows = P("ctx", "fsdp")
    wide = P(None, "fsdp")
    return jax.shard_map(
        shards,
        mesh=mesh,
        in_specs=(rows, rows, rows, rows, rows, wide, wide, wide, P("fsdp"), rows, rows),
        out_specs=(rows, rows, rows, rows, rows, rows, wide, rows),
        check_vma=False,
    )
```

time: 602 us -> 159 us (0.26); the launches traced: 591 us -> 159 us
  waiting for transfers between devices: 391 us -> 0 us
  Pallas kernels: 0 us -> 159 us
  other arithmetic: 82.4 us -> 0 us
  local copies, waits for them, and re-layouts: 57.5 us -> 0 us
  matrix products: 21.8 us -> 0 us
  loops' own time: 17.2 us -> 0 us
  between operations: 14.5 us -> 0.65 us
  starting transfers between devices: 7.24 us -> 0 us
    all_gather x5 -> x0, waiting for transfers between devices: 173 us -> none  [the longest x3 120 us: entering(): everything = jax.tree.map(lambda part: lax.all_gather(part, axis), x)]
    pallas_call x0 -> x2, Pallas kernels: none -> 159 us  [the longest x1 93.8 us: shards(): pl.pallas_call(kernel, out_shape=(block,) * 8, in_specs=[hbm] * len(args)...]
    reduce_scatter x2 -> x0, waiting for transfers between devices: 117 us -> none  [the longest x1 76.7 us: shards(): lax.psum_scatter(lax.dot_general(columns, mixed_li, (((0,), (0,)), ((), (...]
    psum x1 -> x0, waiting for transfers between devices: 98.6 us -> none  [shards(): grad_taps = lax.psum(tap_partial, 'ctx') * grad_scale]
    select_n x64 -> x0, other arithmetic: 50.5 us -> none  [lap(): return jax.tree.map(lambda a, b: jnp.where(reached, a, b), new, before)]
    dynamic_slice x48 -> x0, local copies, waits for them, and re-layouts: 42.7 us -> none  [the longest x32 33.3 us: one_turn(): lax.dynamic_index_in_dim(tap_weights, tap_index, 0, keepdims=False)]
    dot_general x7 -> x0, matrix products: 21.8 us -> none  [the longest x4 8.33 us: emit_block(): jnp.dot(lower, scaled.reshape(block_len, -1), precision=lax.Precision.HIG...]
    another operation x9 -> x0, loops' own time: 17.2 us -> none  [the longest x1 11.4 us: tap_gradient(): stacked = lax.map(one_group, jnp.arange(tap_count // 8, dtype=jnp.int32))]
  transfers between devices with their start and end apart: 10 -> 0, of which waited for: 8 -> 0; matrix products, arithmetic and copies ran while one was open for 17% -> 0% of each run, Pallas kernels for 0% -> 0%
where the time goes in v1:
time: 159 us
  Pallas kernels  159 us (100%)
    pallas_call x1, Pallas kernels, shards(): pl.pallas_call(kernel, out_shape=(block,) * 8, in_specs=[hbm] * len(args)...  93.8 us
    pallas_call x1, Pallas kernels, shards(): pl.pallas_call(write_out, out_shape=(block,) * 8, in_specs=[hbm] * 8, out...  64.7 us

profile of v1, /device:TPU:1, one launch (start us, length us, event | category | flops | bytes accessed | tf_op | source)
XLA Modules:
  0.0 159.2 jit_solution(13697945873661709441)
XLA Ops:
  0.6 93.8 %shard_map.197 = (f32[128,512]{1,0:T(8,128)}, f32[128,512]{1,0:T(8,128)}, f32[128,512]{1,0:T(8,128)}, f32[128,512]{1,0:T(8,128)}, f32[128,512]{1,0:T(8,128)}, /*...) custom-call(bf16[128,512]{1,0:T(8,128)(2,1)} %refs_0_.1, bf16[128,512]{1,0:T(8,128)(2,1)} %refs_1_.1, ...), custom_call_target="tpu_custom_call" | custom-call | flops 3000000000 | bytes 4000000 | tf_op jit(solution)/shard_map/pallas_call | solution.py:765
  94.4 64.7 %shard_map.198 = (f32[128,512]{1,0:T(8,128)}, f32[128,512]{1,0:T(8,128)}, f32[128,512]{1,0:T(8,128)}, f32[128,512]{1,0:T(8,128)}, f32[128,512]{1,0:T(8,128)}, /*...) custom-call(f32[128,512]{1,0:T(8,128)} %get-tuple-element.16.refs_0_, ...), custom_call_target="tpu_custom_call" | custom-call | bytes 4000000 | tf_op jit(solution)/shard_map/pallas_call | solution.py:777

commit v2 on v1

--- a/solution.py
+++ b/solution.py
@@ -82,11 +82,12 @@
 ID_T4 = 48
 ID_SF2 = 49
 ID_SB2 = 65
-ID_D = 81
-ID_T2 = 97
-ID_T3 = 113
-ID_B = 129
-ID_COUNT = 140
+ID_T2 = 81
+ID_T3 = 97
+ID_D1 = 113
+ID_D2 = 129
+ID_B = 133
+ID_COUNT = 149
 
 SCRATCH = dict(
     product=((ROWS, COLS), BF),
@@ -127,10 +128,16 @@
     gm_mate=((ROWS, COLS), F32),
     spec=((2 * ROWS, COLS), F32),
     grad_out=((ROWS, COLS), F32),
-    dw_send=((CHIPS, ROWS, COLS), BF),
-    dw_slots=((CHIPS, ROWS, COLS), BF),
-    o_send=((8, 2 * ROWS, 256), BF),
-    o_slots=((8, 2 * ROWS, 256), BF),
+    dw_part=((CHIPS, ROWS, COLS), BF),
+    dw_half=((RING, ROWS, COLS), BF),
+    dw_from_prev=((RING, ROWS, COLS), BF),
+    dw_from_next=((RING, ROWS, COLS), BF),
+    dw_ring=((RING, ROWS, COLS), BF),
+    dw_half2=((ROWS, COLS), BF),
+    dw_from_prev2=((ROWS, COLS), BF),
+    dw_from_next2=((ROWS, COLS), BF),
+    o_part=((8, 2 * ROWS, 256), BF),
+    o_came=((8, 2 * ROWS, 256), BF),
     o_sum=((2 * ROWS, 256), F32),
     o_mate=((ROWS, 256), F32),
     t_own=((ROWS, COLS), F32),
@@ -564,15 +571,105 @@
         part = lax.dot_general(
             cg[j], s["mixed"][...], (((0,), (0,)), ((), ())), preferred_element_type=F32
         ).astype(BF)
-        s["dw_send"][2 * j] = part[:ROWS]
-        s["dw_send"][2 * j + 1] = part[ROWS:]
+        s["dw_part"][2 * j] = part[:ROWS]
+        s["dw_part"][2 * j + 1] = part[ROWS:]
         return carry
 
     lax.fori_loop(0, n_z, project, 0)
 
-    def d_copy(d):
-        to = chip_off(d)
-        return copy(s["dw_send"].at[to], s["dw_slots"].at[d], ID_D + d, plane(to, k))
+    def dpart(ra, rb):
+        return s["dw_part"].at[at(ring(a, ra), ring(b, rb))]
+
+    def drows(ra, rb, rows):
+        return s["dw_part"].at[at(ring(a, ra), ring(b, rb)), rows]
+
+    def accumulate(target, came):
+        target[...] = (target[...].astype(F32) + came[...].astype(F32)).astype(BF)
+
+    def d_start(j):
+        ra, i = REL[j], ID_D1 + 4 * j
+        send(drows(ra, 2, low), s["dw_half"].at[j, low], i, b_next)
+        send(drows(ra, 2, high), s["dw_half"].at[j, high], i + 1, b_prev)
+
+    def d_middle(j):
+        ra, i = REL[j], ID_D1 + 4 * j
+        arrived(s["dw_half"].at[j, low], i, b_next)
+        accumulate(drows(ra, 1, low), s["dw_half"].at[j, low])
+        send(dpart(ra, 1), s["dw_from_prev"].at[j], i + 2, b_next)
+        arrived(s["dw_half"].at[j, high], i + 1, b_prev)
+        accumulate(drows(ra, -1, high), s["dw_half"].at[j, high])
+        send(dpart(ra, -1), s["dw_from_next"].at[j], i + 3, b_prev)
+
+    def d_sum(j):
+        ra, i = REL[j], ID_D1 + 4 * j
+        arrived(s["dw_from_prev"].at[j], i + 2, b_next)
+        arrived(s["dw_from_next"].at[j], i + 3, b_prev)
+        return (
+            dpart(ra, 0)[...].astype(F32)
+            + s["dw_from_prev"][j].astype(F32)
+            + s["dw_from_next"][j].astype(F32)
+        )
+
+    def d_end(j):
+        s["dw_ring"][j] = d_sum(j).astype(BF)
+
+    def d_turn():
+        send(s["dw_ring"].at[3, low], s["dw_half2"].at[low], ID_D2, a_next)
+        send(s["dw_ring"].at[3, high], s["dw_half2"].at[high], ID_D2 + 1, a_prev)
+
+    def d_turn_middle():
+        arrived(s["dw_half2"].at[low], ID_D2, a_next)
+        accumulate(s["dw_ring"].at[2, low], s["dw_half2"].at[low])
+        send(s["dw_ring"].at[2], s["dw_from_prev2"], ID_D2 + 2, a_next)
+        arrived(s["dw_half2"].at[high], ID_D2 + 1, a_prev)
+        accumulate(s["dw_ring"].at[1, high], s["dw_half2"].at[high])
+        send(s["dw_ring"].at[1], s["dw_from_next2"], ID_D2 + 3, a_prev)
+
+    for j in (3, 2, 1, 0):
+        d_start(j)
+
+    def share(j, carry):
+        block = wg[pl.ds(2 * j, 2)].reshape(2 * ROWS, COLS)
+        s["o_part"][j] = lax.dot_general(
+            s["mixed"][...], block, (((1,), (1,)), ((), ())), preferred_element_type=F32
+        ).astype(BF)
+        return carry
+
+    def opart(dz, chunk):
+        return s["o_part"].at[lax.rem(z + dz + n_z, n_z), pl.ds(chunk * ROWS, ROWS)]
+
+    def ocame(direction, step, chunk):
+        return s["o_came"].at[direction * 4 + step - 1, pl.ds(chunk * ROWS, ROWS)]
+
+    def b_send(direction, step, chunk):
+        dz = (5 - step) * (1 if direction == 0 else -1)
+        send(
+            opart(dz, chunk),
+            ocame(direction, step, chunk),
+            ID_B + direction * 8 + (step - 1) * 2 + chunk,
+            z_next if direction == 0 else z_prev,
+        )
+
+    def b_arrived(direction, step, chunk):
+        arrived(
+            ocame(direction, step, chunk),
+            ID_B + direction * 8 + (step - 1) * 2 + chunk,
+            z_next if direction == 0 else z_prev,
+        )
+
+    def b_start():
+        for direction in range(2):
+            b_send(direction, 1, direction)
+            b_send(direction, 2, 1 - direction)
+
+    def b_forward(step, chunk):
+        for direction in range(2):
+            if step == 1 and chunk != direction:
+                continue
+            b_arrived(direction, step, chunk)
+            dz = (4 - step) * (1 if direction == 0 else -1)
+            accumulate(opart(dz, chunk), ocame(direction, step, chunk))
+            b_send(direction, step + 1, chunk)
 
     def loop(first, count, action):
         def step(d, carry):
@@ -588,33 +685,27 @@
     s["grad_out"][...] = gm * ql[...].astype(F32)
     gather_state(s["grad_out"], s["up0"], s["b_own"], True)
     send(s["b_own"], s["b_mate"], ID_SB1, mate)
-    spectrum = conj_times(s["long_spec"][...], transform(s["grad_out"][...]))
+    lax.fori_loop(0, n_z, share, 0)
+    b_start()
     arrived(s["b_mate"], ID_SB1, mate)
     chip_state(s["b_own"], s["b_mate"], s["b_chip"], s["b_slots"], ID_SB2, ID_SB3, s["b_in"], True)
-    loop(1, CHIPS, lambda d: d_copy(d).start())
-    s["grad_out"][...] = inverse(spectrum) + skip[...] * s["grad_out"][...]
-
-    def o_copy(dz):
-        return copy(s["o_send"].at[dz], s["o_slots"].at[dz], ID_B + dz, up(dz))
-
-    def share(dz, carry):
-        j = lax.rem(z + dz, n_z)
-        block = wg[pl.ds(2 * j, 2)].reshape(2 * ROWS, COLS)
-        s["o_send"][dz] = lax.dot_general(
-            s["mixed"][...], block, (((1,), (1,)), ((), ())), preferred_element_type=F32
-        ).astype(BF)
-        o_copy(dz).start()
-        return carry
-
-    lax.fori_loop(1, n_z, share, 0)
+    d_middle(3)
+    d_middle(2)
     s["o_sum"][...] = lax.dot_general(
         s["mixed"][...],
         wg[pl.ds(2 * z, 2)].reshape(2 * ROWS, COLS),
         (((1,), (1,)), ((), ())),
         preferred_element_type=F32,
     )
-
+    b_forward(1, 0)
+    b_forward(1, 1)
+    d_middle(1)
+    d_middle(0)
+    spectrum = conj_times(s["long_spec"][...], transform(s["grad_out"][...]))
+    s["grad_out"][...] = inverse(spectrum) + skip[...] * s["grad_out"][...]
+    b_forward(2, 0)
     b_sent = chip_finish(s["b_chip"], s["b_slots"], ID_SB2, ID_SB3, s["b_in"], True)
+    b_forward(2, 1)
     arrived(s["b_in"].at[other8], ID_SB3, mate)
     s["enter"][...] = jnp.where(
         k == 1, s["b_in"][...], s["dev_decay"][...] * s["b_in"][...] + s["b_mate"][...]
@@ -645,15 +736,9 @@
         return pl.ds(pl.multiple_of(core * th, th), th)
 
     send(s["t_own"].at[trows(1 - k)], s["t_mate"], ID_T1, mate)
-
-    @pl.when(me == last)
-    def _():
-        s["after"][...] = jnp.zeros((ROWS, COLS), BF)
-
-    @pl.when(me < last)
-    def _():
-        back.wait_recv()
-
+    d_end(3)
+    d_turn()
+    b_forward(3, 0)
     arrived(s["t_mate"], ID_T1, mate)
     s["t_half"][...] = s["t_own"][trows(k), :] + s["t_mate"][...]
 
@@ -668,6 +753,18 @@
         return copy(s["t_half"].at[rows, lanes], s["t_slots"].at[d], ID_T2 + d, plane(to, k))
 
     loop(1, CHIPS, lambda d: t2_copy(d).start())
+    b_forward(3, 1)
+    d_end(2)
+    d_end(1)
+    d_turn_middle()
+
+    @pl.when(me == last)
+    def _():
+        s["after"][...] = jnp.zeros((ROWS, COLS), BF)
+
+    @pl.when(me < last)
+    def _():
+        back.wait_recv()
 
     n = s["after"][...]
     spec = s["spec"][...] - dot(past2[...], jnp.concatenate([n, n], axis=0))
@@ -696,20 +793,16 @@
 
     loop(1, CHIPS, lambda d: t3_copy(d).start())
 
-    loop(1, n_z, lambda d: o_copy(d).wait_recv())
-    total = s["o_sum"][...]
-    for d in range(1, n_z):
-        total = total + s["o_slots"][d].astype(F32)
-    s["o_sum"][...] = total
+    for direction in range(2):
+        for chunk in range(2):
+            b_arrived(direction, 4, chunk)
+    s["o_sum"][...] = s["o_sum"][...] + s["o_came"][3].astype(F32) + s["o_came"][7].astype(F32)
     send(s["o_sum"].at[half(1 - k)], s["o_mate"], ID_OUT, mate)
 
-    loop(1, CHIPS, t3_arrived)
-    send(s["t_all"].at[trows(k)], s["t_all"].at[trows(k)], ID_T4, mate)
-
-    loop(1, CHIPS, lambda d: d_copy(d).wait_recv())
-    total = s["dw_send"][chip].astype(F32)
-    for d in range(1, CHIPS):
-        total = total + s["dw_slots"][d].astype(F32)
+    total = d_sum(0)
+    arrived(s["dw_from_prev2"], ID_D2 + 2, a_next)
+    arrived(s["dw_from_next2"], ID_D2 + 3, a_prev)
+    total = total + s["dw_from_prev2"][...].astype(F32) + s["dw_from_next2"][...].astype(F32)
     gw[...] = total * grad_scale
     store(gw, 7)
 
@@ -721,6 +814,8 @@
         out[:, theirs] = s["o_mate"][:, h * LANES : (h + 1) * LANES]
     store(out, 0)
 
+    loop(1, CHIPS, t3_arrived)
+    send(s["t_all"].at[trows(k)], s["t_all"].at[trows(k)], ID_T4, mate)
     arrived(s["t_all"].at[trows(1 - k)], ID_T4, mate)
     store(s["t_all"], 6)
 
@@ -730,10 +825,8 @@
         c.wait_send()
     f_sent()
     b_sent()
-    loop(1, CHIPS, lambda d: d_copy(d).wait_send())
     loop(1, CHIPS, lambda d: t2_copy(d).wait_send())
     loop(1, CHIPS, lambda d: t3_copy(d).wait_send())
-    loop(1, n_z, lambda d: o_copy(d).wait_send())
 
     @pl.when(me < last)
     def _():
@@ -779,17 +872,26 @@
         out_shape=(block,) * 8,
         in_specs=[hbm] * 8,
         out_specs=(hbm,) * 8,
-        scratch_shapes=[pltpu.SemaphoreType.DMA((8,))],
+        scratch_shapes=[
+            pltpu.VMEM((8, ROWS, COLS), F32),
+            pltpu.SemaphoreType.DMA((8,)),
+            pltpu.SemaphoreType.DMA((8,)),
+        ],
         compiler_params=pltpu.CompilerParams(vmem_limit_bytes=60 * 1024 * 1024),
         cost_estimate=pl.CostEstimate(flops=0, bytes_accessed=4_000_000, transcendentals=0),
     )(*results)
 
 
 def write_out(*refs):
-    copies = [pltpu.make_async_copy(refs[i], refs[8 + i], refs[16].at[i]) for i in range(8)]
-    for c in copies:
+    held, load_sem, store_sem = refs[16:]
+    loads = [pltpu.make_async_copy(refs[i], held.at[i], load_sem.at[i]) for i in range(8)]
+    stores = [pltpu.make_async_copy(held.at[i], refs[8 + i], store_sem.at[i]) for i in range(8)]
+    for c in loads:
         c.start()
-    for c in copies:
+    for load, store in zip(loads, stores):
+        load.wait()
+        store.start()
+    for c in stores:
         c.wait()
 
 

time: 159 us -> 72.9 us (0.46)
  Pallas kernels: 159 us -> 72.1 us
    pallas_call x1, Pallas kernels: 64.7 us -> 2.4 us  [shards(): pl.pallas_call(write_out, out_shape=(block,) * 8, in_specs=[hbm] * 8, out...]
    pallas_call x1, Pallas kernels: 93.8 us -> 69.7 us  [shards(): pl.pallas_call(kernel, out_shape=(block,) * 8, in_specs=[hbm] * len(args)...]
where the time goes in v2:
time: 72.9 us; the launch traced here: 72.8 us
  Pallas kernels  72.1 us (99%)
    pallas_call x1, Pallas kernels, shards(): pl.pallas_call(kernel, out_shape=(block,) * 8, in_specs=[hbm] * len(args)...  69.7 us
    pallas_call x1, Pallas kernels, shards(): pl.pallas_call(write_out, out_shape=(block,) * 8, in_specs=[hbm] * 8, out...  2.4 us

profile of v2, /device:TPU:1, one launch (start us, length us, event | category | flops | bytes accessed | tf_op | source)
XLA Modules:
  0.0 72.8 jit_solution(10300328194319753511)
XLA Ops:
  0.6 69.7 %shard_map.197 = (f32[128,512]{1,0:T(8,128)}, f32[128,512]{1,0:T(8,128)}, f32[128,512]{1,0:T(8,128)}, f32[128,512]{1,0:T(8,128)}, f32[128,512]{1,0:T(8,128)}, /*...) custom-call(bf16[128,512]{1,0:T(8,128)(2,1)} %refs_0_.1, bf16[128,512]{1,0:T(8,128)(2,1)} %refs_1_.1, ...), custom_call_target="tpu_custom_call" | custom-call | flops 3000000000 | bytes 4000000 | tf_op jit(solution)/shard_map/pallas_call | solution.py:858
  70.4 2.4 %shard_map.198 = (f32[128,512]{1,0:T(8,128)}, f32[128,512]{1,0:T(8,128)}, f32[128,512]{1,0:T(8,128)}, f32[128,512]{1,0:T(8,128)}, f32[128,512]{1,0:T(8,128)}, /*...) custom-call(f32[128,512]{1,0:T(8,128)} %get-tuple-element.16.refs_0_, ...), custom_call_target="tpu_custom_call" | custom-call | bytes 4000000 | tf_op jit(solution)/shard_map/pallas_call | solution.py:870

commit v3 on v2

--- a/solution.py
+++ b/solution.py
@@ -1,5 +1,5 @@
-import functools
 import math
+import types
 
 import jax
 import jax.numpy as jnp
@@ -87,7 +87,8 @@
 ID_D1 = 113
 ID_D2 = 129
 ID_B = 133
-ID_COUNT = 149
+ID_CR = 149
+ID_COUNT = 181
 
 SCRATCH = dict(
     product=((ROWS, COLS), BF),
@@ -180,8 +181,8 @@
     results = refs[n_in : n_in + 8]
     held = refs[n_in + 8 : n_in + 8 + n_in]
     (km, vm, cot, w, taps, time, residue, qm, kl, ql, skip, fwd3, past2, inv3) = held
-    s = dict(zip(SCRATCH, refs[2 * n_in + 8 :]))
-    out, gqm, gkm, gvm, gql, gkl, gw = (s[n] for n in ("out", "gqm", "gkm", "gvm", "gql", "gkl", "gw"))
+    s = types.SimpleNamespace(**dict(zip(SCRATCH, refs[2 * n_in + 8 :])))
+    out, gqm, gkm, gvm, gql, gkl, gw = s.out, s.gqm, s.gkm, s.gvm, s.gql, s.gkl, s.gw
     snd, rcv, ld, st = refs[2 * n_in + 8 + len(SCRATCH) :]
 
     def load(i):
@@ -251,11 +252,8 @@
 
     lax.fori_loop(1, CHIPS, greet_chip, 0)
 
-    def greet_z(d, carry):
+    for d in (1, -1):
         pl.semaphore_signal(barrier, inc=1, device_id=up(d), device_id_type=MESH)
-        return carry
-
-    lax.fori_loop(1, n_z, greet_z, 0)
     last = 2 * CHIPS - 1
     across = (me + 2 * k - 1, z)
 
@@ -265,14 +263,14 @@
 
     for i in range(4):
         load(i).wait()
-    s["product"][...] = (km[...].astype(F32) * vm[...].astype(F32)).astype(BF)
+    s.product[...] = (km[...].astype(F32) * vm[...].astype(F32)).astype(BF)
     for h in range(2):
-        s["cg"][z, half(k), h * LANES : (h + 1) * LANES] = cot[
+        s.cg[z, half(k), h * LANES : (h + 1) * LANES] = cot[
             :, pl.ds(pl.multiple_of((2 * h + k) * LANES, LANES), LANES)
         ]
-    s["wg"][chip] = w[...]
-
-    peers = 1 + (CHIPS - 1) + (n_z - 1)
+    s.wg[chip] = w[...]
+
+    peers = 1 + (CHIPS - 1) + 2
 
     @pl.when((me == 0) | (me == last))
     def _():
@@ -285,7 +283,7 @@
     nxt = (lax.rem(me + 1, last + 1), z)
     prv = (lax.rem(me + last, last + 1), z)
 
-    halo = copy(s["product"], s["prev"], ID_HALO, nxt)
+    halo = copy(s.product, s.prev, ID_HALO, nxt)
 
     @pl.when(me < last)
     def _():
@@ -293,61 +291,65 @@
 
     a_next, a_prev = plane(at(ring(a, 1), b), k), plane(at(ring(a, -1), b), k)
     b_next, b_prev = plane(at(a, ring(b, 1)), k), plane(at(a, ring(b, -1)), k)
+    a_over, b_over = plane(at(ring(a, 2), b), k), plane(at(a, ring(b, 2)), k)
     low, high = pl.ds(0, ROWS // 2), pl.ds(ROWS // 2, ROWS // 2)
-    wg = s["wg"]
+    wg = s.wg
 
     def wblock(ra, rb):
         return wg.at[at(ring(a, ra), ring(b, rb))]
 
-    def whalf(ra, rb, rows):
-        return wg.at[at(ring(a, ra), ring(b, rb)), rows]
-
     REL = (0, -1, 1, 2)
 
     def a2_send(j):
         block = wblock(REL[j], 0)
+        if j == 3:
+            send(block, block, ID_A2 + 4 * j + 2, b_over)
         send(block, block, ID_A2 + 4 * j, b_next)
         send(block, block, ID_A2 + 4 * j + 1, b_prev)
 
     def a1_send():
         block = wblock(0, 0)
+        send(block, block, ID_A1 + 2, a_over)
         send(block, block, ID_A1, a_next)
         send(block, block, ID_A1 + 1, a_prev)
 
     def a1_forward():
+        arrived(wblock(1, 0), ID_A1 + 1, a_prev)
+        a2_send(2)
         arrived(wblock(-1, 0), ID_A1, a_next)
-        send(whalf(-1, 0, low), whalf(-1, 0, low), ID_A1 + 2, a_next)
         a2_send(1)
-        arrived(wblock(1, 0), ID_A1 + 1, a_prev)
-        send(whalf(1, 0, high), whalf(1, 0, high), ID_A1 + 3, a_prev)
-        a2_send(2)
 
     def a1_finish():
-        arrived(whalf(2, 0, low), ID_A1 + 2, a_next)
-        arrived(whalf(2, 0, high), ID_A1 + 3, a_prev)
+        arrived(wblock(2, 0), ID_A1 + 2, a_over)
         a2_send(3)
 
     def a2_forward(j):
-        ra = REL[j]
-        arrived(wblock(ra, -1), ID_A2 + 4 * j, b_next)
-        send(whalf(ra, -1, low), whalf(ra, -1, low), ID_A2 + 4 * j + 2, b_next)
-        arrived(wblock(ra, 1), ID_A2 + 4 * j + 1, b_prev)
-        send(whalf(ra, 1, high), whalf(ra, 1, high), ID_A2 + 4 * j + 3, b_prev)
+        block = wblock(REL[j], 1)
+        arrived(block, ID_A2 + 4 * j + 1, b_prev)
+        send(block, block, ID_A2 + 4 * j + 3, b_prev)
 
     def a2_finish(j):
-        ra = REL[j]
-        arrived(whalf(ra, 2, low), ID_A2 + 4 * j + 2, b_next)
-        arrived(whalf(ra, 2, high), ID_A2 + 4 * j + 3, b_prev)
-
-    cg = s["cg"]
+        arrived(wblock(REL[j], -1), ID_A2 + 4 * j, b_next)
+        if j == 3:
+            arrived(wblock(REL[j], 1), ID_A2 + 4 * j + 1, b_prev)
+            arrived(wblock(REL[j], 2), ID_A2 + 4 * j + 2, b_over)
+        else:
+            arrived(wblock(REL[j], 2), ID_A2 + 4 * j + 3, b_prev)
+
+    cg = s.cg
     z_next, z_prev = up(1), up(-1)
 
     def cblock(rz, chunk):
-        rows = half(k) if chunk == 0 else half(1 - k)
+        core = k if chunk < 2 else 1 - k
+        rows = pl.ds(pl.multiple_of(core * ROWS + chunk % 2 * 64, 64), 64)
         return cg.at[lax.rem(z + rz + n_z, n_z), rows]
 
     def c_id(direction, step, chunk):
-        return ID_C + 2 + direction * 8 + (step - 1) * 2 + chunk
+        return ID_CR + direction * 16 + (step - 1) * 4 + chunk
+
+    def c_send(direction, step, chunk):
+        block = cblock(1 - step if direction == 0 else step - 1, chunk)
+        send(block, block, c_id(direction, step, chunk), z_prev if direction else z_next)
 
     def c_mate_refs(h, core):
         return cg.at[z, half(k if core else 1 - k), pl.ds(h * LANES, LANES)]
@@ -360,26 +362,28 @@
                 ID_C + h,
                 mate,
             )
-        send(cblock(0, 0), cblock(0, 0), c_id(0, 1, 0), z_next)
-        send(cblock(0, 0), cblock(0, 0), c_id(1, 1, 0), z_prev)
+        for chunk in range(2):
+            for direction in range(2):
+                c_send(direction, 1, chunk)
 
     def c_second():
         for h in range(2):
             arrived(c_mate_refs(h, False), ID_C + h, mate)
-        send(cblock(0, 1), cblock(0, 1), c_id(0, 1, 1), z_next)
-        send(cblock(0, 1), cblock(0, 1), c_id(1, 1, 1), z_prev)
+        for chunk in (2, 3):
+            for direction in range(2):
+                c_send(direction, 1, chunk)
 
     def c_forward(step, chunk):
-        arrived(cblock(-step, chunk), c_id(0, step, chunk), z_next)
-        if step < 3 or chunk == 0:
-            send(cblock(-step, chunk), cblock(-step, chunk), c_id(0, step + 1, chunk), z_next)
-        arrived(cblock(step, chunk), c_id(1, step, chunk), z_prev)
-        if step < 3 or chunk == 1:
-            send(cblock(step, chunk), cblock(step, chunk), c_id(1, step + 1, chunk), z_prev)
+        for direction in range(2):
+            rz = step if direction else -step
+            arrived(cblock(rz, chunk), c_id(direction, step, chunk), z_prev if direction else z_next)
+            if step < 3 or chunk % 2 == direction:
+                c_send(direction, step + 1, chunk)
 
     def c_finish():
-        arrived(cblock(-4, 0), c_id(0, 4, 0), z_next)
-        arrived(cblock(4, 1), c_id(1, 4, 1), z_prev)
+        for chunk in range(4):
+            direction = chunk % 2
+            arrived(cblock(4, chunk), c_id(direction, 4, chunk), z_prev if direction else z_next)
 
     a1_send()
     c_start()
@@ -398,17 +402,17 @@
         for n in (6, 5, 4, 3, 2):
             series = 1.0 - u * (1.0 / n) * series
         coef = residue[:, lanes] * jnp.sqrt(u * series)
-        s["dev_decay"][:, lanes] = jnp.exp(-rate * ROWS)
-        s["chip_decay"][:, lanes] = jnp.exp(-rate * (2 * ROWS))
+        s.dev_decay[:, lanes] = jnp.exp(-rate * ROWS)
+        s.chip_decay[:, lanes] = jnp.exp(-rate * (2 * ROWS))
         r3 = jnp.broadcast_to(rate[:, None, :], (MODES, 8, LANES))
         c3 = jnp.broadcast_to(coef[:, None, :], (MODES, 8, LANES))
-        s["d8"][:, :, lanes] = jnp.exp(-r3 * 8.0)
+        s.d8[:, :, lanes] = jnp.exp(-r3 * 8.0)
         up0 = jnp.exp(-r3 * within)
-        s["up0"][:, :, lanes] = up0
-        s["up7"][:, :, lanes] = jnp.exp(-r3 * (7.0 - within))
-        s["c0"][:, :, lanes] = c3 * up0
-        s["c1"][:, :, lanes] = c3 * jnp.exp(-r3 * (within + 1.0))
-        s["c8"][:, :, lanes] = c3 * jnp.exp(-r3 * (8.0 - within))
+        s.up0[:, :, lanes] = up0
+        s.up7[:, :, lanes] = jnp.exp(-r3 * (7.0 - within))
+        s.c0[:, :, lanes] = c3 * up0
+        s.c1[:, :, lanes] = c3 * jnp.exp(-r3 * (within + 1.0))
+        s.c8[:, :, lanes] = c3 * jnp.exp(-r3 * (8.0 - within))
         return carry
 
     lax.fori_loop(0, GROUPS, tables, 0)
@@ -416,7 +420,7 @@
     def spread(table, state, target, descending):
         def one(g, carry):
             lanes = pl.ds(pl.multiple_of(g * LANES, LANES), LANES)
-            d8 = s["d8"][:, :, lanes]
+            d8 = s.d8[:, :, lanes]
             v = table[:, :, lanes]
             if state is not None:
                 v = v * jnp.broadcast_to(state[:, lanes][:, None, :], (MODES, 8, LANES))
@@ -432,7 +436,7 @@
     def gather_state(source, table, target, descending):
         def one(g, carry):
             lanes = pl.ds(pl.multiple_of(g * LANES, LANES), LANES)
-            d8 = s["d8"][:, :, lanes]
+            d8 = s.d8[:, :, lanes]
             v = jnp.zeros((MODES, 8, LANES), F32)
             for t in range(ROWS // 8):
                 tile = ROWS // 8 - 1 - t if descending else t
@@ -450,11 +454,15 @@
         return dot(inv3[...], split3(v))
 
     c_second()
-    s["tap_spec"][...] = transform(taps[...])
+    s.tap_spec[...] = transform(taps[...])
+    spread(s.c0, None, s.work, False)
+    c_forward(1, 0)
+    c_forward(1, 1)
     a1_forward()
-    spread(s["c0"], None, s["work"], False)
-    c_forward(1, 0)
-    s["long_spec"][...] = transform(s["work"][...])
+    c_forward(1, 2)
+    a2_forward(0)
+    c_forward(1, 3)
+    s.long_spec[...] = transform(s.work[...])
 
     @pl.when(me > 0)
     def _():
@@ -462,30 +470,30 @@
 
     @pl.when(me == 0)
     def _():
-        s["prev"][...] = jnp.zeros((ROWS, COLS), BF)
+        s.prev[...] = jnp.zeros((ROWS, COLS), BF)
 
     here2 = jnp.concatenate([fwd3[:, :ROWS], fwd3[:, 2 * ROWS :]], axis=1)
-    p, q = s["product"][...], s["prev"][...]
-    s["prod_spec"][...] = dot(here2, jnp.concatenate([p, p], axis=0)) + dot(
+    p, q = s.product[...], s.prev[...]
+    s.prod_spec[...] = dot(here2, jnp.concatenate([p, p], axis=0)) + dot(
         past2[...], jnp.concatenate([q, q], axis=0)
     )
     a1_finish()
-    s["mr_conv"][...] = inverse(times(s["prod_spec"][...], s["tap_spec"][...]))
-    mixed_mr = (qm[...].astype(F32) * s["mr_conv"][...]).astype(BF)
-    s["mixed_mr"][...] = mixed_mr
-    s["signal"][...] = (kl[...].astype(F32) * mixed_mr.astype(F32)).astype(BF).astype(F32)
+    c_forward(2, 0)
+    s.mr_conv[...] = inverse(times(s.prod_spec[...], s.tap_spec[...]))
+    mixed_mr = (qm[...].astype(F32) * s.mr_conv[...]).astype(BF)
+    s.mixed_mr[...] = mixed_mr
+    s.signal[...] = (kl[...].astype(F32) * mixed_mr.astype(F32)).astype(BF).astype(F32)
 
     own8 = pl.ds(pl.multiple_of(k * 8, 8), 8)
 
-    def chip_state(own, theirs, into, slots, id2, id3, target, descending):
-        decay = s["dev_decay"][own8, :]
+    def chip_state(own, theirs, into, slots, id2, descending):
+        decay = s.dev_decay[own8, :]
         mine, other = own[own8, :], theirs[own8, :]
         near = jnp.where(k == 0, mine, other)
         far = jnp.where(k == 0, other, mine)
         into[...] = near + decay * far if descending else decay * near + far
         sign = -1 if descending else 1
         ahead = chip if descending else CHIPS - 1 - chip
-        behind = CHIPS - 1 - chip if descending else chip
 
         def put(d, carry):
             @pl.when(d <= ahead)
@@ -494,7 +502,8 @@
 
             return carry
 
-        lax.fori_loop(1, CHIPS, put, 0)
+        for d in range(1, CHIPS):
+            put(d, 0)
 
     def chip_finish(into, slots, id2, id3, target, descending):
         sign = -1 if descending else 1
@@ -509,7 +518,7 @@
             return carry
 
         lax.fori_loop(1, CHIPS, take, 0)
-        decay = s["chip_decay"][own8, :]
+        decay = s.chip_decay[own8, :]
         total = jnp.zeros((8, COLS), F32)
         for d in range(CHIPS - 1, 0, -1):
             total = jnp.where(d <= behind, total * decay + slots[d], 0.0)
@@ -527,119 +536,118 @@
 
     other8 = pl.ds(pl.multiple_of((1 - k) * 8, 8), 8)
 
-    gather_state(s["signal"], s["up7"], s["f_own"], False)
-    send(s["f_own"], s["f_mate"], ID_SF1, mate)
-    a2_forward(0)
-    c_forward(1, 1)
-    arrived(s["f_mate"], ID_SF1, mate)
-    chip_state(s["f_own"], s["f_mate"], s["f_chip"], s["f_slots"], ID_SF2, ID_SF3, s["f_in"], False)
+    c_forward(2, 1)
+    c_forward(2, 2)
+    gather_state(s.signal, s.up7, s.f_own, False)
+    send(s.f_own, s.f_mate, ID_SF1, mate)
+    c_forward(2, 3)
+    a2_forward(2)
     a2_forward(1)
-    spectrum = times(transform(s["signal"][...]), s["long_spec"][...])
-    s["li_out"][...] = inverse(spectrum) + skip[...] * s["signal"][...]
-    c_forward(2, 0)
-    a2_forward(2)
-    f_sent = chip_finish(s["f_chip"], s["f_slots"], ID_SF2, ID_SF3, s["f_in"], False)
-    c_forward(2, 1)
-    arrived(s["f_in"].at[other8], ID_SF3, mate)
-    s["enter"][...] = jnp.where(
-        k == 0, s["f_in"][...], s["dev_decay"][...] * s["f_in"][...] + s["f_mate"][...]
-    )
-    spread(s["c1"], s["enter"], s["work"], False)
-    s["li_out"][...] = s["li_out"][...] + s["work"][...]
-    s["mixed"][half(k), :] = (ql[...].astype(F32) * s["li_out"][...]).astype(BF)
-    send(s["mixed"].at[half(k)], s["mixed"].at[half(k)], ID_MIX, mate)
-    a2_forward(3)
+    arrived(s.f_mate, ID_SF1, mate)
+    chip_state(s.f_own, s.f_mate, s.f_chip, s.f_slots, ID_SF2, False)
     c_forward(3, 0)
     c_forward(3, 1)
+    spectrum = times(transform(s.signal[...]), s.long_spec[...])
+    c_forward(3, 2)
+    c_forward(3, 3)
+    s.li_out[...] = inverse(spectrum) + skip[...] * s.signal[...]
+
+    f_sent = chip_finish(s.f_chip, s.f_slots, ID_SF2, ID_SF3, s.f_in, False)
+    arrived(s.f_in.at[other8], ID_SF3, mate)
+    s.enter[...] = jnp.where(k == 0, s.f_in[...], s.dev_decay[...] * s.f_in[...] + s.f_mate[...])
+    spread(s.c1, s.enter, s.work, False)
+    s.li_out[...] = s.li_out[...] + s.work[...]
+    s.mixed[half(k), :] = (ql[...].astype(F32) * s.li_out[...]).astype(BF)
+    send(s.mixed.at[half(k)], s.mixed.at[half(k)], ID_MIX, mate)
     for j in range(4):
         a2_finish(j)
     c_finish()
 
-    s["gm_part"][...] = jnp.zeros((2 * ROWS, COLS), F32)
+    s.gm_part[...] = jnp.zeros((2 * ROWS, COLS), F32)
 
     def contract(j, carry):
         block = wg[pl.ds(2 * j, 2)].reshape(2 * ROWS, COLS)
-        s["gm_part"][...] += dot(cg[j], block)
+        s.gm_part[...] += dot(cg[j], block)
         return carry
 
     lax.fori_loop(0, n_z, contract, 0)
-    send(s["gm_part"].at[half(1 - k)], s["gm_mate"], ID_GM, mate)
-
-    arrived(s["mixed"].at[half(1 - k)], ID_MIX, mate)
+    send(s.gm_part.at[half(1 - k)], s.gm_mate, ID_GM, mate)
+
+    arrived(s.mixed.at[half(1 - k)], ID_MIX, mate)
 
     def project(j, carry):
         part = lax.dot_general(
-            cg[j], s["mixed"][...], (((0,), (0,)), ((), ())), preferred_element_type=F32
+            cg[j], s.mixed[...], (((0,), (0,)), ((), ())), preferred_element_type=F32
         ).astype(BF)
-        s["dw_part"][2 * j] = part[:ROWS]
-        s["dw_part"][2 * j + 1] = part[ROWS:]
+        s.dw_part[2 * j] = part[:ROWS]
+        s.dw_part[2 * j + 1] = part[ROWS:]
         return carry
 
     lax.fori_loop(0, n_z, project, 0)
 
     def dpart(ra, rb):
-        return s["dw_part"].at[at(ring(a, ra), ring(b, rb))]
+        return s.dw_part.at[at(ring(a, ra), ring(b, rb))]
 
     def drows(ra, rb, rows):
-        return s["dw_part"].at[at(ring(a, ra), ring(b, rb)), rows]
+        return s.dw_part.at[at(ring(a, ra), ring(b, rb)), rows]
 
     def accumulate(target, came):
         target[...] = (target[...].astype(F32) + came[...].astype(F32)).astype(BF)
 
     def d_start(j):
         ra, i = REL[j], ID_D1 + 4 * j
-        send(drows(ra, 2, low), s["dw_half"].at[j, low], i, b_next)
-        send(drows(ra, 2, high), s["dw_half"].at[j, high], i + 1, b_prev)
+        send(drows(ra, 2, low), s.dw_half.at[j, low], i, b_next)
+        send(drows(ra, 2, high), s.dw_half.at[j, high], i + 1, b_prev)
 
     def d_middle(j):
         ra, i = REL[j], ID_D1 + 4 * j
-        arrived(s["dw_half"].at[j, low], i, b_next)
-        accumulate(drows(ra, 1, low), s["dw_half"].at[j, low])
-        send(dpart(ra, 1), s["dw_from_prev"].at[j], i + 2, b_next)
-        arrived(s["dw_half"].at[j, high], i + 1, b_prev)
-        accumulate(drows(ra, -1, high), s["dw_half"].at[j, high])
-        send(dpart(ra, -1), s["dw_from_next"].at[j], i + 3, b_prev)
+        arrived(s.dw_half.at[j, low], i, b_next)
+        accumulate(drows(ra, 1, low), s.dw_half.at[j, low])
+        send(dpart(ra, 1), s.dw_from_prev.at[j], i + 2, b_next)
+        arrived(s.dw_half.at[j, high], i + 1, b_prev)
+        accumulate(drows(ra, -1, high), s.dw_half.at[j, high])
+        send(dpart(ra, -1), s.dw_from_next.at[j], i + 3, b_prev)
 
     def d_sum(j):
         ra, i = REL[j], ID_D1 + 4 * j
-        arrived(s["dw_from_prev"].at[j], i + 2, b_next)
-        arrived(s["dw_from_next"].at[j], i + 3, b_prev)
+        arrived(s.dw_from_prev.at[j], i + 2, b_next)
+        arrived(s.dw_from_next.at[j], i + 3, b_prev)
         return (
             dpart(ra, 0)[...].astype(F32)
-            + s["dw_from_prev"][j].astype(F32)
-            + s["dw_from_next"][j].astype(F32)
+            + s.dw_from_prev[j].astype(F32)
+            + s.dw_from_next[j].astype(F32)
         )
 
     def d_end(j):
-        s["dw_ring"][j] = d_sum(j).astype(BF)
+        s.dw_ring[j] = d_sum(j).astype(BF)
 
     def d_turn():
-        send(s["dw_ring"].at[3, low], s["dw_half2"].at[low], ID_D2, a_next)
-        send(s["dw_ring"].at[3, high], s["dw_half2"].at[high], ID_D2 + 1, a_prev)
+        send(s.dw_ring.at[3, low], s.dw_half2.at[low], ID_D2, a_next)
+        send(s.dw_ring.at[3, high], s.dw_half2.at[high], ID_D2 + 1, a_prev)
 
     def d_turn_middle():
-        arrived(s["dw_half2"].at[low], ID_D2, a_next)
-        accumulate(s["dw_ring"].at[2, low], s["dw_half2"].at[low])
-        send(s["dw_ring"].at[2], s["dw_from_prev2"], ID_D2 + 2, a_next)
-        arrived(s["dw_half2"].at[high], ID_D2 + 1, a_prev)
-        accumulate(s["dw_ring"].at[1, high], s["dw_half2"].at[high])
-        send(s["dw_ring"].at[1], s["dw_from_next2"], ID_D2 + 3, a_prev)
+        arrived(s.dw_half2.at[low], ID_D2, a_next)
+        accumulate(s.dw_ring.at[2, low], s.dw_half2.at[low])
+        send(s.dw_ring.at[2], s.dw_from_prev2, ID_D2 + 2, a_next)
+        arrived(s.dw_half2.at[high], ID_D2 + 1, a_prev)
+        accumulate(s.dw_ring.at[1, high], s.dw_half2.at[high])
+        send(s.dw_ring.at[1], s.dw_from_next2, ID_D2 + 3, a_prev)
 
     for j in (3, 2, 1, 0):
         d_start(j)
 
     def share(j, carry):
         block = wg[pl.ds(2 * j, 2)].reshape(2 * ROWS, COLS)
-        s["o_part"][j] = lax.dot_general(
-            s["mixed"][...], block, (((1,), (1,)), ((), ())), preferred_element_type=F32
+        s.o_part[j] = lax.dot_general(
+            s.mixed[...], block, (((1,), (1,)), ((), ())), preferred_element_type=F32
         ).astype(BF)
         return carry
 
     def opart(dz, chunk):
-        return s["o_part"].at[lax.rem(z + dz + n_z, n_z), pl.ds(chunk * ROWS, ROWS)]
+        return s.o_part.at[lax.rem(z + dz + n_z, n_z), pl.ds(chunk * ROWS, ROWS)]
 
     def ocame(direction, step, chunk):
-        return s["o_came"].at[direction * 4 + step - 1, pl.ds(chunk * ROWS, ROWS)]
+        return s.o_came.at[direction * 4 + step - 1, pl.ds(chunk * ROWS, ROWS)]
 
     def b_send(direction, step, chunk):
         dz = (5 - step) * (1 if direction == 0 else -1)
@@ -678,47 +686,48 @@
 
         lax.fori_loop(first, count, step, 0)
 
-    arrived(s["gm_mate"], ID_GM, mate)
-    gm = s["gm_part"][half(k), :] + s["gm_mate"][...]
-    gql[...] = gm * s["li_out"][...]
+    arrived(s.gm_mate, ID_GM, mate)
+    gm = s.gm_part[half(k), :] + s.gm_mate[...]
+    s.grad_out[...] = gm * ql[...].astype(F32)
+    gather_state(s.grad_out, s.up0, s.b_own, True)
+    send(s.b_own, s.b_mate, ID_SB1, mate)
+    gql[...] = gm * s.li_out[...]
     store(gql, 4)
-    s["grad_out"][...] = gm * ql[...].astype(F32)
-    gather_state(s["grad_out"], s["up0"], s["b_own"], True)
-    send(s["b_own"], s["b_mate"], ID_SB1, mate)
     lax.fori_loop(0, n_z, share, 0)
     b_start()
-    arrived(s["b_mate"], ID_SB1, mate)
-    chip_state(s["b_own"], s["b_mate"], s["b_chip"], s["b_slots"], ID_SB2, ID_SB3, s["b_in"], True)
+    arrived(s.b_mate, ID_SB1, mate)
+    chip_state(s.b_own, s.b_mate, s.b_chip, s.b_slots, ID_SB2, True)
+    s.spec[...] = conj_times(s.long_spec[...], transform(s.grad_out[...]))
     d_middle(3)
-    d_middle(2)
-    s["o_sum"][...] = lax.dot_general(
-        s["mixed"][...],
+    s.o_sum[...] = lax.dot_general(
+        s.mixed[...],
         wg[pl.ds(2 * z, 2)].reshape(2 * ROWS, COLS),
         (((1,), (1,)), ((), ())),
         preferred_element_type=F32,
     )
+    d_middle(2)
     b_forward(1, 0)
     b_forward(1, 1)
+    s.grad_out[...] = inverse(s.spec[...]) + skip[...] * s.grad_out[...]
     d_middle(1)
     d_middle(0)
-    spectrum = conj_times(s["long_spec"][...], transform(s["grad_out"][...]))
-    s["grad_out"][...] = inverse(spectrum) + skip[...] * s["grad_out"][...]
+
+    b_sent = chip_finish(s.b_chip, s.b_slots, ID_SB2, ID_SB3, s.b_in, True)
     b_forward(2, 0)
-    b_sent = chip_finish(s["b_chip"], s["b_slots"], ID_SB2, ID_SB3, s["b_in"], True)
     b_forward(2, 1)
-    arrived(s["b_in"].at[other8], ID_SB3, mate)
-    s["enter"][...] = jnp.where(
-        k == 1, s["b_in"][...], s["dev_decay"][...] * s["b_in"][...] + s["b_mate"][...]
+    arrived(s.b_in.at[other8], ID_SB3, mate)
+    s.enter[...] = jnp.where(
+        k == 1, s.b_in[...], s.dev_decay[...] * s.b_in[...] + s.b_mate[...]
     )
-    spread(s["c8"], s["enter"], s["work"], True)
-    gli = s["grad_out"][...] + s["work"][...]
-    gkl[...] = gli * s["mixed_mr"][...].astype(F32)
+    spread(s.c8, s.enter, s.work, True)
+    gli = s.grad_out[...] + s.work[...]
+    gkl[...] = gli * s.mixed_mr[...].astype(F32)
     gmm = gli * kl[...].astype(F32)
-    gqm[...] = gmm * s["mr_conv"][...]
+    gqm[...] = gmm * s.mr_conv[...]
     gconv = gmm * qm[...].astype(F32)
-    s["work"][...] = gconv
-    s["grad_halo"][...] = gconv.astype(BF)
-    back = copy(s["grad_halo"], s["after"], ID_BACK_HALO, prv)
+    s.work[...] = gconv
+    s.grad_halo[...] = gconv.astype(BF)
+    back = copy(s.grad_halo, s.after, ID_BACK_HALO, prv)
 
     @pl.when(me > 0)
     def _():
@@ -727,20 +736,17 @@
     store(gkl, 5)
     store(gqm, 1)
 
-    spec = transform(s["work"][...])
-    s["spec"][...] = spec
-    s["t_own"][...] = inverse(conj_times(s["prod_spec"][...], spec))
+    spec = transform(s.work[...])
+    s.spec[...] = spec
+    s.t_own[...] = inverse(conj_times(s.prod_spec[...], spec))
     th = ROWS // 2
 
     def trows(core):
         return pl.ds(pl.multiple_of(core * th, th), th)
 
-    send(s["t_own"].at[trows(1 - k)], s["t_mate"], ID_T1, mate)
-    d_end(3)
-    d_turn()
-    b_forward(3, 0)
-    arrived(s["t_mate"], ID_T1, mate)
-    s["t_half"][...] = s["t_own"][trows(k), :] + s["t_mate"][...]
+    send(s.t_own.at[trows(1 - k)], s.t_mate, ID_T1, mate)
+    arrived(s.t_mate, ID_T1, mate)
+    s.t_half[...] = s.t_own[trows(k), :] + s.t_mate[...]
 
     def piece(c, base):
         rows = pl.ds(pl.multiple_of(base + lax.div(c, 2) * 8, 8), 8)
@@ -750,9 +756,13 @@
     def t2_copy(d):
         to = chip_off(d)
         rows, lanes = piece(to, 0)
-        return copy(s["t_half"].at[rows, lanes], s["t_slots"].at[d], ID_T2 + d, plane(to, k))
-
-    loop(1, CHIPS, lambda d: t2_copy(d).start())
+        return copy(s.t_half.at[rows, lanes], s.t_slots.at[d], ID_T2 + d, plane(to, k))
+
+    for d in range(1, CHIPS):
+        t2_copy(d).start()
+    d_end(3)
+    d_turn()
+    b_forward(3, 0)
     b_forward(3, 1)
     d_end(2)
     d_end(1)
@@ -760,15 +770,15 @@
 
     @pl.when(me == last)
     def _():
-        s["after"][...] = jnp.zeros((ROWS, COLS), BF)
+        s.after[...] = jnp.zeros((ROWS, COLS), BF)
 
     @pl.when(me < last)
     def _():
         back.wait_recv()
 
-    n = s["after"][...]
-    spec = s["spec"][...] - dot(past2[...], jnp.concatenate([n, n], axis=0))
-    gp = inverse(conj_times(s["tap_spec"][...], spec))
+    n = s.after[...]
+    spec = s.spec[...] - dot(past2[...], jnp.concatenate([n, n], axis=0))
+    gp = inverse(conj_times(s.tap_spec[...], spec))
     gkm[...] = gp * vm[...].astype(F32)
     gvm[...] = gp * km[...].astype(F32)
     store(gkm, 2)
@@ -776,48 +786,49 @@
 
     loop(1, CHIPS, lambda d: t2_copy(d).wait_recv())
     rows, lanes = piece(chip, 0)
-    total = s["t_half"][rows, lanes]
+    total = s.t_half[rows, lanes]
     for d in range(1, CHIPS):
-        total = total + s["t_slots"][d]
+        total = total + s.t_slots[d]
     total = total * grad_scale
-    s["t_done"][...] = total
+    s.t_done[...] = total
     rows, lanes = piece(chip, k * th)
-    s["t_all"][rows, lanes] = total
+    s.t_all[rows, lanes] = total
 
     def t3_copy(d):
-        return copy(s["t_done"], s["t_all"].at[rows, lanes], ID_T3 + d, plane(chip_off(d), k))
+        return copy(s.t_done, s.t_all.at[rows, lanes], ID_T3 + d, plane(chip_off(d), k))
 
     def t3_arrived(d):
         rows_from, lanes_from = piece(chip_off(-d), k * th)
-        copy(s["t_done"], s["t_all"].at[rows_from, lanes_from], ID_T3 + d, plane(chip_off(d), k)).wait_recv()
-
-    loop(1, CHIPS, lambda d: t3_copy(d).start())
+        copy(s.t_done, s.t_all.at[rows_from, lanes_from], ID_T3 + d, plane(chip_off(d), k)).wait_recv()
+
+    for d in range(1, CHIPS):
+        t3_copy(d).start()
 
     for direction in range(2):
         for chunk in range(2):
             b_arrived(direction, 4, chunk)
-    s["o_sum"][...] = s["o_sum"][...] + s["o_came"][3].astype(F32) + s["o_came"][7].astype(F32)
-    send(s["o_sum"].at[half(1 - k)], s["o_mate"], ID_OUT, mate)
+    s.o_sum[...] = s.o_sum[...] + s.o_came[3].astype(F32) + s.o_came[7].astype(F32)
+    send(s.o_sum.at[half(1 - k)], s.o_mate, ID_OUT, mate)
 
     total = d_sum(0)
-    arrived(s["dw_from_prev2"], ID_D2 + 2, a_next)
-    arrived(s["dw_from_next2"], ID_D2 + 3, a_prev)
-    total = total + s["dw_from_prev2"][...].astype(F32) + s["dw_from_next2"][...].astype(F32)
+    arrived(s.dw_from_prev2, ID_D2 + 2, a_next)
+    arrived(s.dw_from_next2, ID_D2 + 3, a_prev)
+    total = total + s.dw_from_prev2[...].astype(F32) + s.dw_from_next2[...].astype(F32)
     gw[...] = total * grad_scale
     store(gw, 7)
 
-    arrived(s["o_mate"], ID_OUT, mate)
+    arrived(s.o_mate, ID_OUT, mate)
     for h in range(2):
         mine = pl.ds(pl.multiple_of((2 * h + k) * LANES, LANES), LANES)
         theirs = pl.ds(pl.multiple_of((2 * h + 1 - k) * LANES, LANES), LANES)
-        out[:, mine] = s["o_sum"][half(k), h * LANES : (h + 1) * LANES]
-        out[:, theirs] = s["o_mate"][:, h * LANES : (h + 1) * LANES]
+        out[:, mine] = s.o_sum[half(k), h * LANES : (h + 1) * LANES]
+        out[:, theirs] = s.o_mate[:, h * LANES : (h + 1) * LANES]
     store(out, 0)
 
     loop(1, CHIPS, t3_arrived)
-    send(s["t_all"].at[trows(k)], s["t_all"].at[trows(k)], ID_T4, mate)
-    arrived(s["t_all"].at[trows(1 - k)], ID_T4, mate)
-    store(s["t_all"], 6)
+    send(s.t_all.at[trows(k)], s.t_all.at[trows(k)], ID_T4, mate)
+    arrived(s.t_all.at[trows(1 - k)], ID_T4, mate)
+    store(s.t_all, 6)
 
     for c in stored:
         c.wait()

time: 72.9 us -> 69.7 us (0.956)
  Pallas kernels: 72.1 us -> 68.9 us
    pallas_call x1, Pallas kernels: 69.7 us -> 66.5 us  [shards(): pl.pallas_call(kernel, out_shape=(block,) * 8, in_specs=[hbm] * len(args)...]
where the time goes in v3:
time: 69.7 us; the launch traced here: 69.6 us
  Pallas kernels  68.9 us (99%)
    pallas_call x1, Pallas kernels, shards(): pl.pallas_call(kernel, out_shape=(block,) * 8, in_specs=[hbm] * len(args)...  66.5 us
    pallas_call x1, Pallas kernels, shards(): pl.pallas_call(write_out, out_shape=(block,) * 8, in_specs=[hbm] * 8, out...  2.4 us

profile of v3, /device:TPU:1, one launch (start us, length us, event | category | flops | bytes accessed | tf_op | source)
XLA Modules:
  0.0 69.6 jit_solution(12157756804781699026)
XLA Ops:
  0.6 66.5 %shard_map.197 = (f32[128,512]{1,0:T(8,128)}, f32[128,512]{1,0:T(8,128)}, f32[128,512]{1,0:T(8,128)}, f32[128,512]{1,0:T(8,128)}, f32[128,512]{1,0:T(8,128)}, /*...) custom-call(bf16[128,512]{1,0:T(8,128)(2,1)} %refs_0_.1, bf16[128,512]{1,0:T(8,128)(2,1)} %refs_1_.1, ...), custom_call_target="tpu_custom_call" | custom-call | flops 3000000000 | bytes 4000000 | tf_op jit(solution)/shard_map/pallas_call | solution.py:869
  67.2 2.4 %shard_map.198 = (f32[128,512]{1,0:T(8,128)}, f32[128,512]{1,0:T(8,128)}, f32[128,512]{1,0:T(8,128)}, f32[128,512]{1,0:T(8,128)}, f32[128,512]{1,0:T(8,128)}, /*...) custom-call(f32[128,512]{1,0:T(8,128)} %get-tuple-element.16.refs_0_, ...), custom_call_target="tpu_custom_call" | custom-call | bytes 4000000 | tf_op jit(solution)/shard_map/pallas_call | solution.py:881

commit v4 on v3

--- a/solution.py
+++ b/solution.py
@@ -415,7 +415,7 @@
         s.c8[:, :, lanes] = c3 * jnp.exp(-r3 * (8.0 - within))
         return carry
 
-    lax.fori_loop(0, GROUPS, tables, 0)
+    lax.fori_loop(0, GROUPS, tables, 0, unroll=True)
 
     def spread(table, state, target, descending):
         def one(g, carry):
@@ -431,7 +431,7 @@
                     v = v * d8
             return carry
 
-        lax.fori_loop(0, GROUPS, one, 0)
+        lax.fori_loop(0, GROUPS, one, 0, unroll=True)
 
     def gather_state(source, table, target, descending):
         def one(g, carry):
@@ -445,7 +445,7 @@
             target[:, lanes] = jnp.sum(v * table[:, :, lanes], axis=1)
             return carry
 
-        lax.fori_loop(0, GROUPS, one, 0)
+        lax.fori_loop(0, GROUPS, one, 0, unroll=True)
 
     def transform(v):
         return dot(fwd3[...], split3(v))
@@ -517,7 +517,8 @@
 
             return carry
 
-        lax.fori_loop(1, CHIPS, take, 0)
+        for d in range(1, CHIPS):
+            take(d, 0)
         decay = s.chip_decay[own8, :]
         total = jnp.zeros((8, COLS), F32)
         for d in range(CHIPS - 1, 0, -1):
@@ -563,14 +564,9 @@
         a2_finish(j)
     c_finish()
 
-    s.gm_part[...] = jnp.zeros((2 * ROWS, COLS), F32)
-
-    def contract(j, carry):
-        block = wg[pl.ds(2 * j, 2)].reshape(2 * ROWS, COLS)
-        s.gm_part[...] += dot(cg[j], block)
-        return carry
-
-    lax.fori_loop(0, n_z, contract, 0)
+    s.gm_part[...] = dot(
+        jnp.concatenate([cg[j] for j in range(n_z)], axis=1), wg[...].reshape(CHIPS * ROWS, COLS)
+    )
     send(s.gm_part.at[half(1 - k)], s.gm_mate, ID_GM, mate)
 
     arrived(s.mixed.at[half(1 - k)], ID_MIX, mate)
@@ -583,7 +579,7 @@
         s.dw_part[2 * j + 1] = part[ROWS:]
         return carry
 
-    lax.fori_loop(0, n_z, project, 0)
+    lax.fori_loop(0, n_z, project, 0, unroll=True)
 
     def dpart(ra, rb):
         return s.dw_part.at[at(ring(a, ra), ring(b, rb))]
@@ -680,11 +676,8 @@
             b_send(direction, step + 1, chunk)
 
     def loop(first, count, action):
-        def step(d, carry):
+        for d in range(first, count):
             action(d)
-            return carry
-
-        lax.fori_loop(first, count, step, 0)
 
     arrived(s.gm_mate, ID_GM, mate)
     gm = s.gm_part[half(k), :] + s.gm_mate[...]
@@ -693,7 +686,7 @@
     send(s.b_own, s.b_mate, ID_SB1, mate)
     gql[...] = gm * s.li_out[...]
     store(gql, 4)
-    lax.fori_loop(0, n_z, share, 0)
+    lax.fori_loop(0, n_z, share, 0, unroll=True)
     b_start()
     arrived(s.b_mate, ID_SB1, mate)
     chip_state(s.b_own, s.b_mate, s.b_chip, s.b_slots, ID_SB2, True)

time: 69.7 us -> 66.5 us (0.954)
  Pallas kernels: 68.9 us -> 65.7 us
    pallas_call x1, Pallas kernels: 66.5 us -> 63.3 us  [shards(): pl.pallas_call(kernel, out_shape=(block,) * 8, in_specs=[hbm] * len(args)...]
where the time goes in v4:
time: 66.5 us; the launch traced here: 66.4 us
  Pallas kernels  65.7 us (99%)
    pallas_call x1, Pallas kernels, shards(): pl.pallas_call(kernel, out_shape=(block,) * 8, in_specs=[hbm] * len(args)...  63.3 us
    pallas_call x1, Pallas kernels, shards(): pl.pallas_call(write_out, out_shape=(block,) * 8, in_specs=[hbm] * 8, out...  2.4 us

profile of v4, /device:TPU:1, one launch (start us, length us, event | category | flops | bytes accessed | tf_op | source)
XLA Modules:
  0.0 66.4 jit_solution(14327767133442987744)
XLA Ops:
  0.6 63.3 %shard_map.197 = (f32[128,512]{1,0:T(8,128)}, f32[128,512]{1,0:T(8,128)}, f32[128,512]{1,0:T(8,128)}, f32[128,512]{1,0:T(8,128)}, f32[128,512]{1,0:T(8,128)}, /*...) custom-call(bf16[128,512]{1,0:T(8,128)(2,1)} %refs_0_.1, bf16[128,512]{1,0:T(8,128)(2,1)} %refs_1_.1, ...), custom_call_target="tpu_custom_call" | custom-call | flops 3000000000 | bytes 4000000 | tf_op jit(solution)/shard_map/pallas_call | solution.py:862
  64.0 2.4 %shard_map.198 = (f32[128,512]{1,0:T(8,128)}, f32[128,512]{1,0:T(8,128)}, f32[128,512]{1,0:T(8,128)}, f32[128,512]{1,0:T(8,128)}, f32[128,512]{1,0:T(8,128)}, /*...) custom-call(f32[128,512]{1,0:T(8,128)} %get-tuple-element.16.refs_0_, ...), custom_call_target="tpu_custom_call" | custom-call | bytes 4000000 | tf_op jit(solution)/shard_map/pallas_call | solution.py:874

commit v5 on v4

--- a/solution.py
+++ b/solution.py
@@ -291,7 +291,7 @@
 
     a_next, a_prev = plane(at(ring(a, 1), b), k), plane(at(ring(a, -1), b), k)
     b_next, b_prev = plane(at(a, ring(b, 1)), k), plane(at(a, ring(b, -1)), k)
-    a_over, b_over = plane(at(ring(a, 2), b), k), plane(at(a, ring(b, 2)), k)
+    a_over = plane(at(ring(a, 2), b), k)
     low, high = pl.ds(0, ROWS // 2), pl.ds(ROWS // 2, ROWS // 2)
     wg = s.wg
 
@@ -302,8 +302,6 @@
 
     def a2_send(j):
         block = wblock(REL[j], 0)
-        if j == 3:
-            send(block, block, ID_A2 + 4 * j + 2, b_over)
         send(block, block, ID_A2 + 4 * j, b_next)
         send(block, block, ID_A2 + 4 * j + 1, b_prev)
 
@@ -323,18 +321,27 @@
         arrived(wblock(2, 0), ID_A1 + 2, a_over)
         a2_send(3)
 
+    def whalf(ra, rb, rows):
+        return wg.at[at(ring(a, ra), ring(b, rb)), rows]
+
     def a2_forward(j):
-        block = wblock(REL[j], 1)
-        arrived(block, ID_A2 + 4 * j + 1, b_prev)
-        send(block, block, ID_A2 + 4 * j + 3, b_prev)
+        ra, i = REL[j], ID_A2 + 4 * j
+        arrived(wblock(ra, 1), i + 1, b_prev)
+        if j == 0:
+            send(wblock(ra, 1), wblock(ra, 1), i + 3, b_prev)
+        else:
+            send(whalf(ra, 1, high), whalf(ra, 1, high), i + 3, b_prev)
+            arrived(wblock(ra, -1), i, b_next)
+            send(whalf(ra, -1, low), whalf(ra, -1, low), i + 2, b_next)
 
     def a2_finish(j):
-        arrived(wblock(REL[j], -1), ID_A2 + 4 * j, b_next)
-        if j == 3:
-            arrived(wblock(REL[j], 1), ID_A2 + 4 * j + 1, b_prev)
-            arrived(wblock(REL[j], 2), ID_A2 + 4 * j + 2, b_over)
+        ra, i = REL[j], ID_A2 + 4 * j
+        if j == 0:
+            arrived(wblock(ra, -1), i, b_next)
+            arrived(wblock(ra, 2), i + 3, b_prev)
         else:
-            arrived(wblock(REL[j], 2), ID_A2 + 4 * j + 3, b_prev)
+            arrived(whalf(ra, 2, high), i + 3, b_prev)
+            arrived(whalf(ra, 2, low), i + 2, b_next)
 
     cg = s.cg
     z_next, z_prev = up(1), up(-1)
@@ -548,6 +555,7 @@
     chip_state(s.f_own, s.f_mate, s.f_chip, s.f_slots, ID_SF2, False)
     c_forward(3, 0)
     c_forward(3, 1)
+    a2_forward(3)
     spectrum = times(transform(s.signal[...]), s.long_spec[...])
     c_forward(3, 2)
     c_forward(3, 3)

time: 66.5 us -> 64.7 us (0.973)
  Pallas kernels: 65.7 us -> 63.9 us
    pallas_call x1, Pallas kernels: 63.3 us -> 61.5 us  [shards(): pl.pallas_call(kernel, out_shape=(block,) * 8, in_specs=[hbm] * len(args)...]
where the time goes in v5:
time: 64.7 us; the launch traced here: 64.6 us
  Pallas kernels  63.9 us (99%)
  between operations  0.65 us (1%)
    pallas_call x1, Pallas kernels, shards(): pl.pallas_call(kernel, out_shape=(block,) * 8, in_specs=[hbm] * len(args)...  61.5 us
    pallas_call x1, Pallas kernels, shards(): pl.pallas_call(write_out, out_shape=(block,) * 8, in_specs=[hbm] * 8, out...  2.4 us

profile of v5, /device:TPU:1, one launch (start us, length us, event | category | flops | bytes accessed | tf_op | source)
XLA Modules:
  0.0 64.6 jit_solution(17539015125439739194)
XLA Ops:
  0.6 61.5 %shard_map.197 = (f32[128,512]{1,0:T(8,128)}, f32[128,512]{1,0:T(8,128)}, f32[128,512]{1,0:T(8,128)}, f32[128,512]{1,0:T(8,128)}, f32[128,512]{1,0:T(8,128)}, /*...) custom-call(bf16[128,512]{1,0:T(8,128)(2,1)} %refs_0_.1, bf16[128,512]{1,0:T(8,128)(2,1)} %refs_1_.1, ...), custom_call_target="tpu_custom_call" | custom-call | flops 3000000000 | bytes 4000000 | tf_op jit(solution)/shard_map/pallas_call | solution.py:870
  62.2 2.4 %shard_map.198 = (f32[128,512]{1,0:T(8,128)}, f32[128,512]{1,0:T(8,128)}, f32[128,512]{1,0:T(8,128)}, f32[128,512]{1,0:T(8,128)}, f32[128,512]{1,0:T(8,128)}, /*...) custom-call(f32[128,512]{1,0:T(8,128)} %get-tuple-element.16.refs_0_, ...), custom_call_target="tpu_custom_call" | custom-call | bytes 4000000 | tf_op jit(solution)/shard_map/pallas_call | solution.py:882

commit v6 on v5

--- a/solution.py
+++ b/solution.py
@@ -555,10 +555,10 @@
     chip_state(s.f_own, s.f_mate, s.f_chip, s.f_slots, ID_SF2, False)
     c_forward(3, 0)
     c_forward(3, 1)
-    a2_forward(3)
     spectrum = times(transform(s.signal[...]), s.long_spec[...])
     c_forward(3, 2)
     c_forward(3, 3)
+    a2_forward(3)
     s.li_out[...] = inverse(spectrum) + skip[...] * s.signal[...]
 
     f_sent = chip_finish(s.f_chip, s.f_slots, ID_SF2, ID_SF3, s.f_in, False)

time: 64.7 us -> 64.5 us (level)
  no operation moved by 1% of the time
where the time goes in v6:
time: 64.5 us; the launch traced here: 64.4 us
  Pallas kernels  63.7 us (99%)
  between operations  0.65 us (1%)
    pallas_call x1, Pallas kernels, shards(): pl.pallas_call(kernel, out_shape=(block,) * 8, in_specs=[hbm] * len(args)...  61.4 us
    pallas_call x1, Pallas kernels, shards(): pl.pallas_call(write_out, out_shape=(block,) * 8, in_specs=[hbm] * 8, out...  2.4 us

profile of v6, /device:TPU:1, one launch (start us, length us, event | category | flops | bytes accessed | tf_op | source)
XLA Modules:
  0.0 64.4 jit_solution(9938676398384146945)
XLA Ops:
  0.6 61.4 %shard_map.197 = (f32[128,512]{1,0:T(8,128)}, f32[128,512]{1,0:T(8,128)}, f32[128,512]{1,0:T(8,128)}, f32[128,512]{1,0:T(8,128)}, f32[128,512]{1,0:T(8,128)}, /*...) custom-call(bf16[128,512]{1,0:T(8,128)(2,1)} %refs_0_.1, bf16[128,512]{1,0:T(8,128)(2,1)} %refs_1_.1, ...), custom_call_target="tpu_custom_call" | custom-call | flops 3000000000 | bytes 4000000 | tf_op jit(solution)/shard_map/pallas_call | solution.py:870
  62.0 2.4 %shard_map.198 = (f32[128,512]{1,0:T(8,128)}, f32[128,512]{1,0:T(8,128)}, f32[128,512]{1,0:T(8,128)}, f32[128,512]{1,0:T(8,128)}, f32[128,512]{1,0:T(8,128)}, /*...) custom-call(f32[128,512]{1,0:T(8,128)} %get-tuple-element.16.refs_0_, ...), custom_call_target="tpu_custom_call" | custom-call | bytes 4000000 | tf_op jit(solution)/shard_map/pallas_call | solution.py:882
